TPU v7x, 32 devices: a whole 2x2x4 slice. The times are simulated.
32 devices in a mesh: seq: 4 (over z), fsdp: 8 (over y, x, core).
Axes of the slice: x: 2, y: 2, z: 4, core: 2. Of those that a mesh axis runs over, the one named last changes fastest.
Arguments:
- tokens: bfloat16 [8, 4096, 1024], P('fsdp', 'seq'), may hold values from -6 to 6
- norm_gain: float32 [1024], replicated, may hold values from 0.25 to 1.75
- in_weight: bfloat16 [1024, 4384], P('fsdp'), may hold values from -0.1875 to 0.1875
- conv_weight: float32 [4, 2304], replicated, may hold values from -3 to 3
- conv_bias: float32 [2304], replicated, may hold values from -3 to 3
- dt_bias: float32 [32], replicated, may hold values from -7 to -2
- a_log: float32 [32], replicated, may hold values from -0.5 to 2.8
- skip_gain: float32 [32], replicated, may hold values from 0.5 to 1.5
- gate_gain: float32 [2048], replicated, may hold values from 0.25 to 1.75
- out_weight: bfloat16 [2048, 1024], P('fsdp'), may hold values from -0.125 to 0.125
- cotangent: bfloat16 [8, 4096, 1024], P('fsdp', 'seq'), may hold values from -6 to 6
Outputs:
- mixed: bfloat16 [8, 4096, 1024], P('fsdp', 'seq')
- grad_tokens: float32 [8, 4096, 1024], P('fsdp', 'seq')
- grad_in_weight: float32 [1024, 4384], P(('seq', 'fsdp'))
- grad_out_weight: float32 [2048, 1024], P(('seq', 'fsdp'))
- grad_norm_gain: float32 [1024], replicated
- grad_conv_weight: float32 [4, 2304], replicated
- grad_conv_bias: float32 [2304], replicated
- grad_dt_bias: float32 [32], replicated
- grad_a_log: float32 [32], replicated
- grad_skip_gain: float32 [32], replicated
- grad_gate_gain: float32 [2048], replicated
All inputs are finite; a program needn't handle non-finite values.
Results may differ from a plain program's by a relative error of at most 0.0088.
Values may be sent and summed in bfloat16 or wider, within the bound.
No kernel may reach another device: no remote copies, remote signals or barrier semaphores. Data moves between devices by JAX's collectives and lax.ppermute only.
A program may use at most 448 MiB of HBM per device.

v0:
```python
import jax
import jax.numpy as jnp
from jax import lax
from jax.sharding import PartitionSpec as P

BLOCK = 256


epsilon = 1e-05
highest = lax.Precision.HIGHEST


def from_behind(block, axis, distance):
    devices = range(lax.axis_size(axis))
    route = [(i - distance, i) for i in devices if i - distance in devices]
    return lax.ppermute(block, axis, route)


def first_norm(residual, gain_vector):
    return (
        residual
        * lax.rsqrt(jnp.mean(residual * residual, axis=1, keepdims=True) + epsilon)
        * gain_vector
    )


def gate_norm(mixer_out, gate_in, gain_vector):
    gated_out = mixer_out * jax.nn.silu(gate_in)
    return (
        gated_out
        * lax.rsqrt(jnp.mean(gated_out * gated_out, axis=1, keepdims=True) + epsilon)
        * gain_vector
    )


def block_mixer(values, step_sizes, decay_rates, inputs, outputs, skip_terms, start_state):
    row_count = step_sizes.shape[0]
    head_count = step_sizes.shape[1]
    head_width = values.shape[1] // head_count
    state_width = inputs.shape[1]
    blocks = row_count // BLOCK
    value_blocks = values.reshape(blocks, BLOCK, head_count, head_width)
    step_blocks = step_sizes.reshape(blocks, BLOCK, head_count)
    input_blocks = inputs.reshape(blocks, BLOCK, state_width)
    output_blocks = outputs.reshape(blocks, BLOCK, state_width)
    within = jnp.cumsum(step_blocks * decay_rates, axis=1)
    totals = within[:, -1, :]
    before = jnp.cumsum(totals, axis=0) - totals
    scores = jnp.einsum("cqn,csn->cqs", output_blocks, input_blocks, precision=highest)
    causal = lax.broadcasted_iota(jnp.int32, (BLOCK, BLOCK), 0) >= lax.broadcasted_iota(
        jnp.int32, (BLOCK, BLOCK), 1
    )
    spread = within[:, :, None, :] - within[:, None, :, :]
    decays = jnp.exp(jnp.where(causal[None, :, :, None], spread, -jnp.inf))
    weighted = scores[:, :, :, None] * decays * step_blocks[:, None, :, :]
    inside = jnp.einsum("cqsh,cshp->cqhp", weighted, value_blocks, precision=highest)
    tail_weight = jnp.exp(totals[:, None, :] - within) * step_blocks
    block_states = jnp.einsum(
        "csh,csn,cshp->chpn", tail_weight, input_blocks, value_blocks, precision=highest
    )
    earlier_mask = lax.broadcasted_iota(jnp.int32, (blocks, blocks), 0) > lax.broadcasted_iota(
        jnp.int32, (blocks, blocks), 1
    )
    block_gap = before[:, None, :] - before[None, :, :] - totals[None, :, :]
    block_links = jnp.exp(jnp.where(earlier_mask[:, :, None], block_gap, -jnp.inf))
    entering = jnp.einsum("kjh,jhpn->khpn", block_links, block_states, precision=highest)
    entering = entering + jnp.exp(before)[:, :, None, None] * start_state[None]
    across = (
        jnp.einsum("cqn,chpn->cqhp", output_blocks, entering, precision=highest)
        * jnp.exp(within)[:, :, :, None]
    )
    result = inside + across + skip_terms[None, None, :, None] * value_blocks
    return result.reshape(row_count, head_count * head_width)


def head_groups(values, step_sizes, decay_rates, inputs, outputs, skip_terms, start_state):
    row_count = step_sizes.shape[0]
    head_count = step_sizes.shape[1]
    head_width = values.shape[1] // head_count
    group_size = min(8, head_count)
    group_count = head_count // group_size
    grouped_values = values.reshape(row_count, group_count, group_size * head_width).transpose(
        1, 0, 2
    )
    grouped_steps = step_sizes.reshape(row_count, group_count, group_size).transpose(1, 0, 2)

    def one_group(group_item):
        part_values, part_steps, part_rates, part_skips, part_start = group_item
        return block_mixer(
            part_values, part_steps, part_rates, inputs, outputs, part_skips, part_start
        )

    results = lax.map(
        jax.checkpoint(one_group),
        (
            grouped_values,
            grouped_steps,
            decay_rates.reshape(group_count, group_size),
            skip_terms.reshape(group_count, group_size),
            start_state.reshape(group_count, group_size, head_width, inputs.shape[1]),
        ),
    )
    return results.transpose(1, 0, 2).reshape(row_count, head_count * head_width)


def local(
    tokens,
    norm_gain,
    in_weight,
    conv_weight,
    conv_bias,
    dt_bias,
    a_log,
    skip_gain,
    gate_gain,
    out_weight,
    cotangent,
):
    residual = tokens[0].astype(jnp.float32)
    row_count = residual.shape[0]
    model_width = residual.shape[1]
    head_count = a_log.shape[0]
    inner_width = out_weight.shape[1] * 0 + 2 * model_width
    conv_span = conv_weight.shape[0]
    mixed_width = conv_weight.shape[1]
    state_width = (mixed_width - inner_width) // 2
    head_width = inner_width // head_count
    full_in, full_out = (
        lax.all_gather(in_weight, "fsdp", axis=0, tiled=True),
        lax.all_gather(out_weight, "fsdp", axis=0, tiled=True),
    )
    normed_f, pull_norm = jax.vjp(first_norm, residual, norm_gain)
    normed = normed_f.astype(jnp.bfloat16)
    projected = jnp.dot(normed, full_in, preferred_element_type=jnp.float32)
    gate_in = projected[:, :inner_width]
    conv_in = projected[:, inner_width : inner_width + mixed_width].astype(jnp.bfloat16)
    raw_steps = projected[:, inner_width + mixed_width :]
    rim_rows = from_behind(conv_in[row_count - (conv_span - 1) :], "seq", 1)
    padded = jnp.concatenate([rim_rows, conv_in], axis=0).astype(jnp.float32)
    conv_out = conv_bias + jnp.zeros((row_count, mixed_width), jnp.float32)
    for offset in range(conv_span):
        conv_out = conv_out + conv_weight[offset] * padded[offset : offset + row_count]
    activated = jax.nn.silu(conv_out)
    soft_in = raw_steps + dt_bias
    decay_rates = -jnp.exp(a_log)
    local_heads = head_count // lax.axis_size("seq")
    first_head = lax.axis_index("seq") * local_heads
    values = activated[:, :inner_width].astype(jnp.bfloat16)
    shared = activated[:, inner_width:].astype(jnp.bfloat16)
    step_sizes = jax.nn.softplus(soft_in).astype(jnp.bfloat16)
    head_values, head_steps = (
        lax.all_to_all(values, "seq", split_axis=1, concat_axis=0, tiled=True),
        lax.all_to_all(step_sizes, "seq", split_axis=1, concat_axis=0, tiled=True),
    )
    all_shared = lax.all_gather(shared, "seq", axis=0, tiled=True)
    local_rates = lax.dynamic_slice_in_dim(decay_rates, first_head, local_heads)
    local_skips = lax.dynamic_slice_in_dim(skip_gain, first_head, local_heads)
    zero_start = jnp.zeros((local_heads, head_width, state_width), jnp.float32)

    def regrouped(part_values, part_steps, part_rates, part_shared, part_skips):
        return head_groups(
            part_values,
            part_steps,
            part_rates,
            part_shared[:, :state_width],
            part_shared[:, state_width:],
            part_skips,
            zero_start,
        )

    head_out, pull_mixer = jax.vjp(
        regrouped,
        head_values.astype(jnp.float32),
        head_steps.astype(jnp.float32),
        local_rates,
        all_shared.astype(jnp.float32),
        local_skips,
    )
    mixer_out = lax.all_to_all(
        head_out.astype(jnp.bfloat16), "seq", split_axis=0, concat_axis=1, tiled=True
    ).astype(jnp.float32)
    normed_mix, pull_gate = jax.vjp(gate_norm, mixer_out, gate_in, gate_gain)
    out_in = normed_mix.astype(jnp.bfloat16)
    branch = jnp.dot(out_in, full_out, preferred_element_type=jnp.float32)
    mixed = (residual + branch).astype(jnp.bfloat16)
    incoming = cotangent[0]
    grad_normed_mix = lax.dot_general(
        incoming, full_out, (((1,), (1,)), ((), ())), preferred_element_type=jnp.float32
    )
    grad_mixer, grad_gate_in, grad_gate_gain = pull_gate(grad_normed_mix)
    grad_heads = lax.all_to_all(
        grad_mixer.astype(jnp.bfloat16), "seq", split_axis=1, concat_axis=0, tiled=True
    )
    grad_values_head, grad_steps_head, grad_rates_local, grad_shared_head, grad_skips_local = (
        pull_mixer(grad_heads.astype(jnp.float32))
    )
    grad_values_back, grad_steps_back = (
        lax.all_to_all(
            grad_values_head.astype(jnp.bfloat16), "seq", split_axis=0, concat_axis=1, tiled=True
        ),
        lax.all_to_all(
            grad_steps_head.astype(jnp.bfloat16), "seq", split_axis=0, concat_axis=1, tiled=True
        ),
    )
    grad_shared = lax.psum_scatter(
        grad_shared_head.astype(jnp.bfloat16), "seq", scatter_dimension=0, tiled=True
    ).astype(jnp.float32)
    grad_values = grad_values_back.astype(jnp.float32)
    grad_steps = grad_steps_back.astype(jnp.float32)
    grad_rates = lax.dynamic_update_slice_in_dim(
        jnp.zeros((head_count,), jnp.float32), grad_rates_local, first_head, 0
    )
    grad_skips = lax.dynamic_update_slice_in_dim(
        jnp.zeros((head_count,), jnp.float32), grad_skips_local, first_head, 0
    )
    grad_raw = grad_steps * jax.nn.sigmoid(soft_in)
    grad_dt_bias = jnp.sum(grad_raw, axis=0)
    grad_a_log = grad_rates * decay_rates
    grad_activated = jnp.concatenate([grad_values, grad_shared], axis=1)
    sigmoid_out = jax.nn.sigmoid(conv_out)
    grad_conv = grad_activated * sigmoid_out * (1.0 + conv_out * (1.0 - sigmoid_out))
    grad_conv_bias = jnp.sum(grad_conv, axis=0)
    grad_conv_weight = jnp.stack(
        [
            jnp.sum(padded[offset : offset + row_count] * grad_conv, axis=0)
            for offset in range(conv_span)
        ]
    )
    grad_padded = jnp.zeros((row_count + conv_span - 1, mixed_width), jnp.float32)
    for offset in range(conv_span):
        grad_padded = grad_padded + jnp.pad(
            conv_weight[offset] * grad_conv, ((offset, conv_span - 1 - offset), (0, 0))
        )
    returned = from_behind(grad_padded[: conv_span - 1], "seq", -1)
    grad_conv_in = grad_padded[conv_span - 1 :] + jnp.concatenate(
        [jnp.zeros((row_count - conv_span + 1, mixed_width), jnp.float32), returned], axis=0
    )
    grad_projected = jnp.concatenate([grad_gate_in, grad_conv_in, grad_raw], axis=1).astype(
        jnp.bfloat16
    )
    grad_normed = lax.dot_general(
        grad_projected, full_in, (((1,), (1,)), ((), ())), preferred_element_type=jnp.float32
    )
    grad_residual, grad_norm_gain = pull_norm(grad_normed)
    grad_tokens = (incoming.astype(jnp.float32) + grad_residual)[None]
    own_rows = model_width // (lax.axis_size("seq") * lax.axis_size("fsdp"))
    part_in = lax.dot_general(
        normed, grad_projected, (((0,), (0,)), ((), ())), preferred_element_type=jnp.float32
    )
    part_out = lax.dot_general(
        out_in, incoming, (((0,), (0,)), ((), ())), preferred_element_type=jnp.float32
    )
    summed = lax.psum_scatter(
        jnp.concatenate(
            [part_in, part_out.reshape(lax.axis_size(("seq", "fsdp")) * own_rows, 2 * model_width)],
            axis=1,
        ),
        ("seq", "fsdp"),
        scatter_dimension=0,
        tiled=True,
    )
    proj_width = grad_projected.shape[1]
    grad_in_weight = summed[:, :proj_width]
    grad_out_weight = summed[:, proj_width:].reshape(2 * summed.shape[0], model_width)
    small_sums = lax.psum(
        (
            grad_norm_gain,
            grad_conv_weight,
            grad_conv_bias,
            grad_dt_bias,
            grad_a_log,
            grad_skips,
            grad_gate_gain,
        ),
        ("seq", "fsdp"),
    )
    return (
        mixed[None],
        grad_tokens,
        grad_in_weight,
        grad_out_weight,
        small_sums[0],
        small_sums[1],
        small_sums[2],
        small_sums[3],
        small_sums[4],
        small_sums[5],
        small_sums[6],
    )


def solution(mesh):
    placed = (
        P("fsdp", "seq", None),
        P(),
        P("fsdp", None),
        P(),
        P(),
        P(),
        P(),
        P(),
        P(),
        P("fsdp", None),
        P("fsdp", "seq", None),
    )
    return jax.shard_map(
        local,
        mesh=mesh,
        in_specs=placed,
        out_specs=(
            P("fsdp", "seq", None),
            P("fsdp", "seq", None),
            P(("seq", "fsdp"), None),
            P(("seq", "fsdp"), None),
            P(),
            P(),
            P(),
            P(),
            P(),
            P(),
            P(),
        ),
        check_vma=False,
    )
```

profile of v0, /device:TPU:0, one launch (start us, length us, event | category | flops | bytes accessed | tf_op | source)
XLA Modules:
  0.0 1475.7 jit_solution(3073616327067458633)
XLA Ops:
  11.7 59.5 %all-gather.4.cloned.1.call-done = bf16[1024,4384]{0,1:T(8,128)(2,1)} async-done(((bf16[128,4384]{0,1:T(8,128)(2,1)}), bf16[1024,4384]{0,1:T(8,128)(2,1)}) %all-gather.4.cloned.1.call-update) | async-done | bytes 8978448 | tf_op jit(solution)/shard_map/all_gather | solution.py:129
  71.2 16.3 %fusion.170 = (bf16[1024,4384]{0,1:T(8,128)(2,1)S(1)}, f32[1024,4384]{0,1:T(8,128)}) fusion(bf16[1024,4384]{0,1:T(8,128)(2,1)} %all-gather.4.cloned.1.call-done, bf16[1,1024,1024]{2,1,0:T(8,128)(2,1)} %param.11, f32[1024]{0:T(1024)} %param.12, f32[1024]{0:T(1024)S(1)} %fusion.153), kind=kOutput, calls=%fused_computation.236 | convolution fusion | flops 9202597888 | bytes 38019072 | tf_op jit(solution)/shard_map/dot_general | solution.py:134
  158.3 60.1 %all-gather.6.cloned.1.call-done = bf16[4096,256]{0,1:T(8,128)(2,1)} async-done(((bf16[1024,256]{0,1:T(8,128)(2,1)}), bf16[4096,256]{0,1:T(8,128)(2,1)}) %all-gather.6.cloned.1.call-update) | async-done | bytes 2097168 | tf_op jit(solution)/shard_map/all_gather | solution.py:155
  223.4 42.5 %all-to-all-done = bf16[1024,4,512]{2,0,1:T(8,128)(2,1)} async-done(((bf16[1024,4,512]{2,0,1:T(8,128)(2,1)}), bf16[1024,4,512]{2,0,1:T(8,128)(2,1)}, u32[]{:S(2)}, u32[]{:S(2)}) %all-to-all-start) | async-done | bytes 4194336 | tf_op jit(solution)/shard_map/all_to_all | solution.py:152
  293.0 26.6 %fusion.5 = f32[16,8,64,256]{3,2,1,0:T(8,128)} fusion(bf16[16,256,8,64]{1,3,2,0:T(8,128)(2,1)S(1)} %copy-done.7, f32[16,256,8]{1,2,0:T(8,128)S(1)} %bitcast.312, f32[16,256,8]{1,2,0:T(8,128)S(1)} %copy-done.20, f32[16,256,256]{2,1,0:T(8,128)S(1)} %copy-done.16, pred[256,256]{1,0:T(8,128)(4,1)S(1)} %copy-done.31), kind=kOutput, calls=%fused_computation.9 | convolution fusion | flops 6476005376 | bytes 17104896 | tf_op jit(solution)/shard_map/jvp()/while/body/eval_jaxpr/cqsh,cshp->cqhp/dot_general | solution.py:56
  358.1 91.9 %all-to-all-done.2 = bf16[4,1024,512]{1,2,0:T(8,128)(2,1)} async-done(((bf16[4,1024,512]{1,2,0:T(8,128)(2,1)}), bf16[4,1024,512]{1,2,0:T(8,128)(2,1)}, u32[]{:S(2)}, u32[]{:S(2)}) %all-to-all-start.2) | async-done | bytes 4194336 | tf_op jit(solution)/shard_map/all_to_all | solution.py:179
  466.4 13.1 fusion.31
  500.3 83.6 %all-to-all-done.3 = bf16[1024,4,512]{2,0,1:T(8,128)(2,1)} async-done(((bf16[1024,4,512]{2,0,1:T(8,128)(2,1)}), bf16[1024,4,512]{2,0,1:T(8,128)(2,1)}, u32[]{:S(2)}, u32[]{:S(2)}) %all-to-all-start.3) | async-done | bytes 4194336 | tf_op jit(solution)/shard_map/all_to_all | solution.py:191
  697.4 12.8 fusion.43
  739.8 58.8 %fusion.12 = (f32[16,256,8]{1,2,0:T(8,128)}, f32[16,256,8]{1,2,0:T(8,128)}, f32[16,256,8]{1,2,0:T(8,128)S(1)}, f32[16,256,256]{2,1,0:T(8,128)}) fusion(f32[16,256,8]{1,2,0:T(8,128)S(1)} %bitcast.315, f32[16,256,8]{1,2,0:T(8,128)S(1)} %get-tuple-element.197, f32[16,256,256]{2,1,0:T(8,128)S(1)} %fusion.172, pred[256,256]{1,0:T(8,128)(4,1)S(1)} %copy-done.31, ...), kind=kOutput, calls=%fused_computation.17 | convolution fusion | flops 6550355968 | bytes 25886720 | tf_op jit(solution)/shard_map/transpose(jvp())/while/body/eval_jaxpr/checkpoint/cqsh,cshp->cqhp/dot_general | solution.py:56
  798.7 35.9 %fusion.32 = bf16[16,256,8,64]{1,3,2,0:T(8,128)(2,1)} fusion(f32[16,256,8,64]{1,3,2,0:T(8,128)S(1)} %bitcast.293, f32[16,256,8,64]{1,0,3,2:T(8,128)S(1)} %bitcast.286, f32[16,256,8]{1,2,0:T(8,128)S(1)} %get-tuple-element.215, f32[8]{0:T(128)S(1)} %copy-done.46, f32[16,256,8]{1,2,0:T(8,128)S(1)} %bitcast.316, f32[16,256,8]{1,2,0:T(8,128)S(1)} %get-tuple-element.197, ...), kind=kOutput, calls=%fused_computation.53 | convolution fusion | flops 6486491136 | bytes 34013216 | tf_op jit(solution)/shard_map/transpose(jvp())/while/body/eval_jaxpr/checkpoint/cqsh,cshp->cqhp/dot_general | solution.py:56
  835.4 13.9 multiply_reduce_fusion.8
  849.5 39.6 %reduce-window.26 = f32[16,8,2,128]{3,1,2,0:T(8,128)S(1)} reduce-window(f32[16,8,2,128]{3,1,2,0:T(8,128)S(1)} %add_bitcast_fusion, f32[]{:T(128)} %constant.91.clone.1), window={size=1x1x1x128 pad=0_0x0_0x0_0x0_127}, to_apply=%region_20.21 | reduce-window | flops 4161536 | bytes 262148 | tf_op jit(solution)/shard_map/reduce-window.4
  894.6 25.1 %fusion.38 = f32[16,256,128,1]{2,1,3,0:T(8,128)} fusion(f32[16,256,8,64]{1,0,3,2:T(8,128)} %copy-done.1, f32[8,64,128,16]{2,3,1,0:T(8,128)} %fusion.62, f32[8,64,128]{2,1,0:T(8,128)S(1)} %squeeze.42, f32[16,8]{1,0:T(8,128)S(1)} %get-tuple-element.192), kind=kOutput, calls=%fused_computation.77 | convolution fusion | flops 3223322624 | bytes 14942720 | tf_op jit(solution)/shard_map/transpose(jvp())/while/body/eval_jaxpr/checkpoint/cqn,chpn->cqhp/dot_general | solution.py:69
  952.6 20.6 %fusion.42 = f32[16,256,128,1]{2,1,3,0:T(8,128)S(1)} fusion(f32[16,256,8,64]{1,0,3,2:T(8,128)} %bitcast.276, f32[16,256,8]{1,2,0:T(8,128)S(1)} %get-tuple-element.215, f32[16,8,64,128]{3,0,2,1:T(8,128)} %copy-done.6), kind=kOutput, calls=%fused_computation.81 | convolution fusion | flops 3223322624 | bytes 14811136 | tf_op jit(solution)/shard_map/transpose(jvp())/while/body/eval_jaxpr/checkpoint/csh,csn,cshp->chpn/dot_general | solution.py:58
  1019.3 39.1 %reduce-scatter.5.cloned.1.call-done = bf16[1024,256]{0,1:T(8,128)(2,1)} async-done(((bf16[4096,256]{0,1:T(8,128)(2,1)}), bf16[1024,256]{0,1:T(8,128)(2,1)}) %reduce-scatter.5.cloned.1.call-update) | async-done | bytes 524304 | tf_op jit(solution)/shard_map/reduce_scatter | solution.py:205
  1068.6 27.5 %multiply_reduce_fusion.4 = (f32[2304]{0:T(1024)S(1)}, f32[2304]{0:T(1024)S(1)}, f32[2304]{0:T(1024)S(1)}, f32[2304]{0:T(1024)S(1)}, f32[2304]{0:T(1024)S(1)}, /*index=5*/f32[1024,2304]{0,1:T(8,128)}) fusion(f32[1027,2304]{0,1:T(8,128)} %copy-done, f32[1024,2304]{0,1:T(8,128)} %get-tuple-element.201, bf16[1024,256]{0,1:T(8,128)(2,1)} %reduce-scatter.5.cloned.1.call-done, ...), kind=kLoop, calls=%fused_computation.40 | loop fusion | flops 49533696 | bytes 61387776 | tf_op jit(solution)/shard_map/reduce_sum | solution.py:225
  1117.1 19.6 %pad_add_fusion = f32[1027,2304]{0,1:T(8,128)} fusion(f32[1024,2304]{0,1:T(8,128)} %copy-done.3, f32[1024,2304]{0,1:T(8,128)} %get-tuple-element.207, f32[1024,2304]{0,1:T(8,128)} %get-tuple-element.208, f32[1024,2304]{0,1:T(8,128)} %copy-done.2), kind=kLoop, calls=%fused_computation.32 | loop fusion | flops 7098624 | bytes 47213568 | tf_op jit(solution)/shard_map/add | solution.py:231
  1145.6 19.1 %fusion.70 = f32[1024,4384]{0,1:T(8,128)} fusion(bf16[1024,32]{0,1:T(8,128)(2,1)S(1)} %get-tuple-element.190, bf16[1024,2304]{0,1:T(8,128)(2,1)} %fusion.25, bf16[1024,2048]{0,1:T(8,128)(2,1)} %get-tuple-element.202, bf16[1,1024,1024]{2,1,0:T(8,128)(2,1)S(1)} %copy-done.15, f32[1024]{0:T(1024)S(1)} %copy-done.42, f32[1024]{0:T(1024)S(1)} %copy-done.35), kind=kOutput, calls=%fused_computation.121 | convolution fusion | flops 9225043968 | bytes 29040640 | tf_op jit(solution)/shard_map/dot_general | solution.py:247
  1164.7 19.5 %pad_maximum_fusion = f32[1024,6432]{0,1:T(8,128)} fusion(f32[1024,2048]{0,1:T(8,128)} %copy.444, f32[1024,4384]{0,1:T(8,128)} %fusion.70), kind=kLoop, calls=%fused_computation.15 | loop fusion | flops 6586368 | bytes 52690944 | tf_op jit(solution)/shard_map/concatenate | solution.py:254
  1184.2 27.0 %copy.494 = f32[1024,6432]{1,0:T(8,128)} copy(f32[1024,6432]{0,1:T(8,128)} %pad_maximum_fusion) | data formatting | bytes 52690944
  1229.9 18.3 %fusion.47 = (f32[1024]{0:T(1024)S(1)}, f32[1024]{0:T(1024)S(1)}, f32[1024,1024]{1,0:T(8,128)}) fusion(bf16[1,1024,1024]{2,1,0:T(8,128)(2,1)S(1)} %copy-done.15, f32[1024]{0:T(1024)S(1)} %copy-done.35, f32[1024]{0:T(1024)S(1)} %copy-done.42, bf16[1024,4384]{0,1:T(8,128)(2,1)} %all-gather.4.cloned.1.call-done, bf16[1024,32]{0,1:T(8,128)(2,1)S(1)} %get-tuple-element.190, ...), kind=kOutput, calls=%fused_computation.92 | convolution fusion | flops 9228187648 | bytes 24264704 | tf_op jit(solution)/shard_map/dot_general | solution.py:241
  1248.3 42.1 %all-reduce.8 = (f32[1024]{0:T(1024)}, f32[4,2304]{1,0:T(4,128)}, f32[2304]{0:T(1024)}, f32[32]{0:T(128)}, f32[32]{0:T(128)}, /*index=5*/f32[32]{0:T(128)}, f32[2048]{0:T(1024)}) all-reduce(f32[1024]{0:T(1024)S(1)} %get-tuple-element.174, f32[4,2304]{1,0:T(4,128)S(1)} %pad_maximum_fusion.4, ...), channel_id=1, replica_groups=mesh['seq'=4,'fsdp'=8] {'seq','fsdp'}, use_global_device_ids=true, to_apply=%region_25.26 | all-reduce | flops 14688 | bytes 117504 | tf_op jit(solution)/shard_map/psum | solution.py:265
  1295.2 170.0 %reduce-scatter.7.cloned.1.call-done = f32[32,6432]{1,0:T(8,128)} async-done(((f32[1024,6432]{1,0:T(8,128)}), f32[32,6432]{1,0:T(8,128)}) %reduce-scatter.7.cloned.1.call-update) | async-done | bytes 823312
  (291 shorter events, 478.1 us)
Async XLA Ops:
  7.2 64.0 %all-gather.4.cloned.1.call-start = ((), (), s32[]{:S(2)}) async-start(), calls=%async_computation.8 | async-start | bytes 10100736 | tf_op jit(solution)/shard_map/all_gather | solution.py:129
  8.9 101.8 %copy-start.23 = (f32[2304]{0:T(1024)}, f32[2304]{0:T(1024)S(1)}, u32[]{:S(2)}) copy-start(f32[2304]{0:T(1024)S(1)} %get-tuple-element.178) | copy-start | bytes 27652
  9.0 101.8 %copy-start.25 = (f32[2304]{0:T(1024)}, f32[2304]{0:T(1024)S(1)}, u32[]{:S(2)}) copy-start(f32[2304]{0:T(1024)S(1)} %get-tuple-element.179) | copy-start | bytes 27652
  9.0 101.8 %copy-start.27 = (f32[2304]{0:T(1024)}, f32[2304]{0:T(1024)S(1)}, u32[]{:S(2)}) copy-start(f32[2304]{0:T(1024)S(1)} %get-tuple-element.180) | copy-start | bytes 27652
  9.0 101.8 %copy-start.29 = (f32[2304]{0:T(1024)}, f32[2304]{0:T(1024)S(1)}, u32[]{:S(2)}) copy-start(f32[2304]{0:T(1024)S(1)} %get-tuple-element.181) | copy-start | bytes 27652
  11.7 75.9 %copy-start.34 = (f32[1024]{0:T(1024)}, f32[1024]{0:T(1024)S(1)}, u32[]{:S(2)}) copy-start(f32[1024]{0:T(1024)S(1)} %fusion.153) | copy-start | bytes 12292
  11.7 83.3 %copy-start.43 = (f32[32]{0:T(128)S(1)}, f32[32]{0:T(128)}, u32[]{:S(2)}) copy-start(f32[32]{0:T(128)} %param.16) | copy-start | bytes 388
  91.6 14.0 collective-permute-start
  101.7 31.8 %all-to-all-start.1 = ((bf16[1024,4,8]{0,2,1:T(8,128)(2,1)}), bf16[1024,4,8]{0,2,1:T(8,128)(2,1)S(1)}, u32[]{:S(2)}, u32[]{:S(2)}) async-start(bf16[1024,4,8]{0,2,1:T(8,128)(2,1)} %fusion.130), calls=%async_computation.1 | async-start | bytes 131072 | tf_op jit(solution)/shard_map/all_to_all | solution.py:153
  133.5 132.4 %all-to-all-start = ((bf16[1024,4,512]{2,0,1:T(8,128)(2,1)}), bf16[1024,4,512]{2,0,1:T(8,128)(2,1)}, u32[]{:S(2)}, u32[]{:S(2)}) async-start(bf16[1024,4,512]{2,0,1:T(8,128)(2,1)} %copy.361), calls=%async_computation | async-start | bytes 8388608 | tf_op jit(solution)/shard_map/all_to_all | solution.py:152
  139.0 79.4 %all-gather.6.cloned.1.call-start = ((), (), s32[]{:S(2)}) async-start(), calls=%async_computation.9 | async-start | bytes 2621440 | tf_op jit(solution)/shard_map/all_gather | solution.py:155
  352.5 97.5 %all-to-all-start.2 = ((bf16[4,1024,512]{1,2,0:T(8,128)(2,1)}), bf16[4,1024,512]{1,2,0:T(8,128)(2,1)}, u32[]{:S(2)}, u32[]{:S(2)}) async-start(bf16[4,1024,512]{1,2,0:T(8,128)(2,1)} %copy.385), calls=%async_computation.2 | async-start | bytes 8388608 | tf_op jit(solution)/shard_map/all_to_all | solution.py:179
  357.3 98.7 %copy-start.19 = (bf16[1,1024,1024]{2,1,0:T(8,128)(2,1)S(1)}, bf16[1,1024,1024]{2,1,0:T(8,128)(2,1)}, u32[]{:S(2)}) copy-start(bf16[1,1024,1024]{2,1,0:T(8,128)(2,1)} %param.21) | copy-start | bytes 6291460
  357.3 98.7 %copy-start.38 = (f32[2048]{0:T(1024)S(1)}, f32[2048]{0:T(1024)}, u32[]{:S(2)}) copy-start(f32[2048]{0:T(1024)} %param.19) | copy-start | bytes 24580
  357.3 98.7 %all-gather.8.cloned.1.call-start = ((), (), s32[]{:S(2)}) async-start(), calls=%async_computation.10 | async-start | bytes 4718592 | tf_op jit(solution)/shard_map/all_gather | solution.py:130
  485.8 98.0 %all-to-all-start.3 = ((bf16[1024,4,512]{2,0,1:T(8,128)(2,1)}), bf16[1024,4,512]{2,0,1:T(8,128)(2,1)}, u32[]{:S(2)}, u32[]{:S(2)}) async-start(bf16[1024,4,512]{2,0,1:T(8,128)(2,1)} %copy.387), calls=%async_computation.3 | async-start | bytes 8388608 | tf_op jit(solution)/shard_map/all_to_all | solution.py:191
  500.3 90.2 %copy-start.40 = (f32[8]{0:T(128)S(1)}, f32[8]{0:T(128)}, u32[]{:S(2)}) copy-start(f32[8]{0:T(128)} %copy-done.39) | copy-start | bytes 100
  733.8 64.9 %slice-start.2 = ((s8[8388608]{0:T(1024)(128)(4,1)}), s8[4194304]{0:T(1024)(128)(4,1)S(1)}, s32[]{:S(2)}) async-start(s8[8388608]{0:T(1024)(128)(4,1)} %bitcast.284), calls=%async_computation.15 | async-start | bytes 8388608
  733.8 64.9 %slice-start.4 = ((s8[8388608]{0:T(1024)(128)(4,1)}), s8[4194304]{0:T(1024)(128)(4,1)S(1)}, s32[]{:S(2)}) async-start(s8[8388608]{0:T(1024)(128)(4,1)} %bitcast.292), calls=%async_computation.17 | async-start | bytes 8388608
  890.9 46.5 %all-to-all-start.5 = ((bf16[4,1024,8]{1,2,0:T(8,128)(2,1)}), bf16[4,1024,8]{1,2,0:T(8,128)(2,1)S(1)}, u32[]{:S(2)}, u32[]{:S(2)}) async-start(bf16[4,1024,8]{1,2,0:T(8,128)(2,1)} %bitcast.80), calls=%async_computation.6 | async-start | bytes 131072 | tf_op jit(solution)/shard_map/all_to_all | solution.py:201
  937.4 131.3 %all-to-all-start.4 = ((bf16[4,1024,512]{1,2,0:T(8,128)(2,1)}), bf16[4,1024,512]{1,2,0:T(8,128)(2,1)}, u32[]{:S(2)}, u32[]{:S(2)}) async-start(bf16[4,1024,512]{1,2,0:T(8,128)(2,1)} %copy.411), calls=%async_computation.4 | async-start | bytes 8388608 | tf_op jit(solution)/shard_map/all_to_all | solution.py:198
  942.4 116.1 %reduce-scatter.5.cloned.1.call-start = ((), (), s32[]{:S(2)}) async-start(), calls=%async_computation.11 | async-start | bytes 2621440 | tf_op jit(solution)/shard_map/reduce_scatter | solution.py:205
  987.6 477.5 %reduce-scatter.7.cloned.1.call-start = ((), (), s32[]{:S(2)}) async-start(), calls=%async_computation.12 | async-start | bytes 27574272
  1115.8 20.9 %collective-permute-start.1 = (f32[3,2304]{1,0:T(4,128)S(1)}, f32[3,2304]{1,0:T(4,128)S(1)}, u32[]{:S(2)}, u32[]{:S(2)}) collective-permute-start(f32[3,2304]{1,0:T(4,128)S(1)} %copy.426), channel_id=1, source_target_pairs={{8,0},{16,8},{24,16},{9,1},{17,9},{25,17},{10,2},{18,10},{26,18},{... | collective-permute-start | bytes 82952 | tf_op jit(solution)/shard_map/ppermute | solution.py:16
  (46 other events, 818.1 us)
Sparse Core Ops, SparseCore 0:
  9.9 61.2 all-gather.3
  142.0 76.3 all-gather.5
  360.1 37.1 all-gather.7
  987.8 70.6 reduce-scatter.4
  1211.3 253.8 reduce-scatter.6
where the time goes:
time: 1490 us; the launch traced here: 1480 us
  waiting for transfers between devices  558 us (37%)
  matrix products  372 us (25%)
  other arithmetic  235 us (16%)
  local copies, waits for them, and re-layouts  221 us (15%)
  blocking collectives  42.1 us (3%)
  starting transfers between devices  33.1 us (2%)
  between operations  15 us (1%)
    unnamed x6, waiting for transfers between devices  171 us
    dot_general x3, matrix products, block_mixer(): jnp.einsum('cqsh,cshp->cqhp', weighted, value_blocks, precision=highest)  121 us
    another operation x13, other arithmetic  92.2 us
    all_to_all x1, waiting for transfers between devices, local(): lax.all_to_all(head_out.astype(jnp.bfloat16), 'seq', split_axis=0, concat...  91.9 us
    all_to_all x1, waiting for transfers between devices, local(): lax.all_to_all(grad_mixer.astype(jnp.bfloat16), 'seq', split_axis=1, conc...  83.6 us
    unnamed x121, local copies, waits for them, and re-layouts  71.7 us
    dot_general x4, matrix products, block_mixer(): jnp.einsum('cqn,chpn->cqhp', output_blocks, entering, precision=highest)  60.6 us
    all_gather x1, waiting for transfers between devices, local(): all_shared = lax.all_gather(shared, 'seq', axis=0, tiled=True)  60.1 us
  transfers between devices with their start and end apart: 13, of which 8 were waited for; matrix products, arithmetic and copies ran while one was open for 17% of the time, Pallas kernels for 0%

commit v1 on v0

v1 whole, which is shorter than its diff:
```python
import functools

import jax
import jax.numpy as jnp
from jax import lax
from jax.experimental import pallas as pl
from jax.experimental.pallas import tpu as pltpu
from jax.sharding import PartitionSpec as P

ROWS = 128
LANES = 128
HALO = 16
VMEM = 48 * 1024 * 1024
LOG2E = 1.4426950408889634
epsilon = 1e-05
bf16 = jnp.bfloat16
f32 = jnp.float32
highest = lax.Precision.HIGHEST


def shifted(block, axis, distance):
    size = lax.axis_size(axis)
    route = [(i - distance, i) for i in range(size) if 0 <= i - distance < size]
    return lax.ppermute(block, axis, route)


def exchanged(block, axis, bit):
    return lax.ppermute(block, axis, [(i, i ^ bit) for i in range(lax.axis_size(axis))])


def pick(block, at, axis):
    return lax.dynamic_index_in_dim(block, at, axis, keepdims=False)


def line_sum(part):
    pieces = lax.axis_size("seq")
    me = lax.axis_index("seq")
    up = jnp.zeros_like(part[0])
    down = up
    for t in range(1, pieces):
        ahead = pick(part, jnp.clip(pieces - t + me, 0, pieces - 1), 0)
        behind = pick(part, jnp.clip(t - pieces + me, 0, pieces - 1), 0)
        up = lax.ppermute(up + ahead, "seq", [(i, i + 1) for i in range(t)])
        down = lax.ppermute(down + behind, "seq", [(pieces - 1 - i, pieces - 2 - i) for i in range(t)])
    return pick(part, me, 0).astype(f32) + up.astype(f32) + down.astype(f32)


def sum_all(vector):
    for axis in ("fsdp", "seq"):
        size = lax.axis_size(axis)
        if size & (size - 1):
            vector = lax.psum(vector, axis)
            continue
        for bit in range(size.bit_length() - 1):
            vector = vector + exchanged(vector, axis, 1 << bit)
    return vector


def sum_scatter(part, rows):
    pieces, group = lax.axis_size("seq"), lax.axis_size("fsdp")
    bits = group.bit_length() - 1
    columns = part.shape[1]
    if group != 1 << bits or bits < 1 or pieces > 8 or rows % 2:
        return lax.psum_scatter(part.astype(f32), ("seq", "fsdp"), scatter_dimension=0, tiled=True)
    me = lax.axis_index("fsdp")

    def halve(block, bit, axis):
        mine = (me >> bit) & 1
        got = exchanged(pick(block, 1 - mine, axis), "fsdp", 1 << bit)
        return pick(block, mine, axis) + got

    block = halve(part.reshape(pieces, group // 2, 2, rows, columns), 0, 2)
    halves = []
    for way in (0, 1):
        half = block[:, :, way * (rows // 2) : (way + 1) * (rows // 2)]
        half = half.reshape((pieces,) + (2,) * (bits - 1) + half.shape[2:])
        left = list(range(bits - 1, 0, -1))
        for bit in list(left) if way else left[::-1]:
            half = halve(half, bit, 1 + left.index(bit))
            left.remove(bit)
        halves.append(half)
    return line_sum(jnp.concatenate(halves, axis=1))


def mm(a, b):
    return lax.dot_general(a, b, (((1,), (0,)), ((), ())), preferred_element_type=f32)


def mm_nt(a, b):
    return lax.dot_general(a, b, (((1,), (1,)), ((), ())), preferred_element_type=f32)


def mm_tn(a, b):
    return lax.dot_general(a, b, (((0,), (0,)), ((), ())), preferred_element_type=f32)


def sigmoid(v):
    return 0.5 + 0.5 * jnp.tanh(0.5 * v)


def rows_at():
    return lax.broadcasted_iota(jnp.int32, (ROWS, LANES), 0)


def lanes_at():
    return lax.broadcasted_iota(jnp.int32, (ROWS, LANES), 1)


def slab(i):
    return slice(i * LANES, (i + 1) * LANES)


def wide(i):
    return slice(i * 2 * LANES, (i + 1) * 2 * LANES)


def halves(columns, heads):
    lane = lanes_at()
    high = columns.astype(bf16).astype(f32)
    rest = pltpu.roll(columns - high, heads, 1)
    return jnp.where(lane < heads, high, jnp.where(lane < 2 * heads, rest, 0.0)).astype(bf16)


def low_lanes():
    return (lanes_at() < LANES // 2).astype(f32).astype(bf16), (lanes_at() >= LANES // 2).astype(f32).astype(bf16)


def diagonal(block, low, high):
    return jnp.concatenate([block * low, block * high], axis=0)


def params(**more):
    return pltpu.CompilerParams(vmem_limit_bytes=VMEM, **more)


def cost(microseconds):
    return pl.CostEstimate(flops=int(microseconds * 1e9), bytes_accessed=4 * 1024 * 1024, transcendentals=0)


def whole(shape):
    return pl.BlockSpec(shape, lambda i: (0,) * len(shape))


def by_rows(width, rows=ROWS):
    return pl.BlockSpec((rows, width), lambda i: (i, 0))


def conv_kernel(span, rows, normed_ref, weight_ref, taps_ref, bias_ref, act_ref, cin_ref, held):
    part = 256
    bounds = [(0, HALO)] + [(HALO + at, part) for at in range(0, rows, part)]
    for start, size in bounds:
        block = mm(normed_ref[start : start + size, :], weight_ref[...]).astype(bf16)
        cin_ref[start : start + size, :] = block
        held[start : start + size, :] = block.astype(f32)
    for at in range(0, rows, part):
        total = jnp.broadcast_to(bias_ref[0:1, :], (part, bias_ref.shape[1]))
        for k in range(span):
            start = HALO + at - (span - 1) + k
            total = total + taps_ref[k : k + 1, :] * held[start : start + part, :]
        act_ref[at : at + part, :] = (total * sigmoid(total)).astype(bf16)


def conv_forward(normed, weight, taps, bias):
    rows, width = normed.shape[0] - HALO, normed.shape[1]
    channels = taps.shape[1]
    cols = 256
    return pl.pallas_call(
        functools.partial(conv_kernel, taps.shape[0], rows),
        grid=(channels // cols,),
        in_specs=[
            whole((rows + HALO, width)),
            pl.BlockSpec((width, cols), lambda i: (0, i)),
            pl.BlockSpec((taps.shape[0], cols), lambda i: (0, i)),
            pl.BlockSpec((1, cols), lambda i: (0, i)),
        ],
        out_specs=[
            pl.BlockSpec((rows, cols), lambda i: (0, i)),
            pl.BlockSpec((rows + HALO, cols), lambda i: (0, i)),
        ],
        out_shape=[
            jax.ShapeDtypeStruct((rows, channels), bf16),
            jax.ShapeDtypeStruct((rows + HALO, channels), bf16),
        ],
        scratch_shapes=[pltpu.VMEM((rows + HALO, cols), f32)],
        compiler_params=params(),
        name="conv_forward",
        cost_estimate=cost(14),
    )(normed, weight, taps, bias)


def steps_kernel(blocks, heads, raw_ref, bias_ref, alog_ref, step_ref, cum_ref, left_ref, right_ref, rows3):
    lane = lanes_at()
    lower = (rows_at() >= lane).astype(f32)
    rates = -jnp.exp(alog_ref[...])
    rows3[...] = jnp.zeros_like(rows3)
    for b in range(blocks):
        rows = slice(b * ROWS, (b + 1) * ROWS)
        soft = raw_ref[rows, :] + bias_ref[...]
        soft = jnp.maximum(soft, 0.0) + jnp.log1p(jnp.exp(-jnp.abs(soft)))
        step = soft.astype(bf16).astype(f32)
        step_ref[rows, :] = step
        cum = jnp.dot(lower, step * rates, precision=highest, preferred_element_type=f32)
        cum_ref[rows, :] = cum
        cum = cum * LOG2E
        parts, rest = [], cum
        for _ in range(3):
            part = rest.astype(bf16).astype(f32)
            parts.append(part)
            rest = rest - part
        left = jnp.where(lane < 3 * heads + 3, 1.0, 0.0)
        for k in (2, 1, 0):
            left = jnp.where(lane < (k + 1) * heads, pltpu.roll(parts[k], k * heads, 1), left)
        left_ref[rows, :] = left.astype(bf16)
        for k in range(3):
            flipped = -parts[k].T
            for h in range(heads):
                rows3[k : k + 1, slab(h)] = flipped[h : h + 1, :]
        right_ref[b * HALO : (b + 1) * HALO, :] = rows3[...].astype(bf16)


def steps_forward(raw, bias, a_log, heads):
    rows = raw.shape[0]
    blocks = rows // ROWS
    shape = jax.ShapeDtypeStruct((rows, LANES), f32)
    return pl.pallas_call(
        functools.partial(steps_kernel, blocks, heads),
        out_shape=[
            shape,
            shape,
            jax.ShapeDtypeStruct((rows, LANES), bf16),
            jax.ShapeDtypeStruct((blocks * HALO, heads * LANES), bf16),
        ],
        scratch_shapes=[pltpu.VMEM((HALO, heads * LANES), f32)],
        compiler_params=params(),
        name="steps_forward",
        cost_estimate=cost(6),
    )(raw, bias, a_log)


def state_kernel(heads, v_ref, b_ref, step_ref, cum_ref, etot_ref, fan_ref, x_ref, f_ref, state, tails, both):
    at = pl.program_id(0)

    @pl.when(at == 0)
    def _():
        state[...] = jnp.zeros_like(state)

    cum, step = cum_ref[...], step_ref[...]
    tail = jnp.exp(cum[ROWS - 1 :, :] - cum) * step
    both[...] = mm(jnp.concatenate([halves(step, heads), halves(tail, heads)], axis=0), fan_ref[...])
    v = v_ref[...].astype(f32)
    x_ref[...] = (v * both[:ROWS, :]).astype(bf16)
    tails[...] = (v * both[ROWS:, :]).astype(bf16)
    state[...] = etot_ref[pl.ds(at, 1), :] * state[...] + mm_tn(b_ref[...], tails[...])

    @pl.when(at == pl.num_programs(0) - 1)
    def _():
        f_ref[...] = state[...].astype(bf16)


def piece_state(act, step, cum, etot, fan, heads, inner, width):
    rows = act.shape[0]
    inputs_at = inner // width
    return pl.pallas_call(
        functools.partial(state_kernel, heads),
        grid=(rows // ROWS,),
        in_specs=[
            by_rows(inner),
            pl.BlockSpec((ROWS, width), lambda i: (i, inputs_at)),
            by_rows(LANES),
            by_rows(LANES),
            whole(etot.shape),
            whole(fan.shape),
        ],
        out_specs=[by_rows(inner), whole((width, inner))],
        out_shape=[
            jax.ShapeDtypeStruct((rows, inner), bf16),
            jax.ShapeDtypeStruct((width, inner), bf16),
        ],
        scratch_shapes=[
            pltpu.VMEM((width, inner), f32),
            pltpu.VMEM((ROWS, inner), bf16),
            pltpu.VMEM((2 * ROWS, inner), f32),
        ],
        compiler_params=params(),
        name="piece_state",
        cost_estimate=cost(6),
    )(act, act, step, cum, etot, fan)


def inside_kernel(pairs, x_ref, b_ref, c_ref, left_ref, right_ref, still_ref, y_ref, right):
    fixed = left_rows(right, still_ref, right_ref)
    low, high = low_lanes()
    scores = jnp.where(rows_at() >= lanes_at(), mm_nt(c_ref[...], b_ref[...]), 0.0)
    scores = jnp.concatenate([scores, scores], axis=1)
    left = left_ref[...]
    for i in range(pairs):
        spread = mm(left, fixed[:, wide(i)])
        weights = (scores * jnp.exp2(jnp.minimum(spread, 0.0))).astype(bf16)
        y_ref[:, slab(i)] = mm(weights, diagonal(x_ref[:, slab(i)], low, high)).astype(bf16)


def left_rows(right, still_ref, right_ref):
    @pl.when(pl.program_id(0) == 0)
    def _():
        right[...] = still_ref[...]

    own = still_ref.shape[0] - 2 * HALO
    right[own : own + HALO, :] = right_ref[...]
    return right


def inside_forward(x, act, left, right, still, inner, width):
    rows = act.shape[0]
    inputs_at = inner // width
    return pl.pallas_call(
        functools.partial(inside_kernel, inner // LANES),
        grid=(rows // ROWS,),
        in_specs=[
            by_rows(inner),
            pl.BlockSpec((ROWS, width), lambda i: (i, inputs_at)),
            pl.BlockSpec((ROWS, width), lambda i: (i, inputs_at + 1)),
            by_rows(LANES),
            by_rows(right.shape[1], HALO),
            whole(still.shape),
        ],
        out_specs=by_rows(inner),
        out_shape=jax.ShapeDtypeStruct((rows, inner), bf16),
        scratch_shapes=[pltpu.VMEM(still.shape, bf16)],
        compiler_params=params(),
        name="inside_forward",
        cost_estimate=cost(10),
    )(x, act, act, left, right, still)


def gate_kernel(
    heads,
    pairs,
    y_ref,
    v_ref,
    b_ref,
    c_ref,
    z_ref,
    gn_ref,
    step_ref,
    cum_ref,
    etot_ref,
    ebef_ref,
    skip_ref,
    gain_ref,
    start_ref,
    ones_ref,
    fan_ref,
    out_ref,
    gm_ref,
    gz_ref,
    states_ref,
    pac_ref,
    back_ref,
    ggain_ref,
    gskip_ref,
    state,
    back,
    across,
    mixer,
    gated,
    early,
    tails,
    products,
    both,
):
    at = pl.program_id(0)
    width = pairs * LANES

    @pl.when(at == 0)
    def _():
        state[...] = start_ref[...]
        back[...] = jnp.zeros_like(back)
        ggain_ref[...] = jnp.zeros_like(ggain_ref)
        gskip_ref[...] = jnp.zeros_like(gskip_ref)

    entering = state[...].astype(bf16)
    states_ref[...] = entering
    across[...] = mm(c_ref[...], entering)
    cum = cum_ref[...]
    grow = jnp.exp(cum)
    tail = jnp.exp(cum[ROWS - 1 :, :] - cum) * step_ref[...]
    both[...] = mm(jnp.concatenate([halves(grow, heads), halves(tail, heads)], axis=0), fan_ref[...])
    squares = jnp.zeros((ROWS, LANES), f32)
    meets = jnp.zeros((ROWS, LANES), f32)
    for i in range(pairs):
        s = slab(i)
        v = v_ref[:, s].astype(f32)
        ya = across[:, s] * both[:ROWS, s]
        across[:, s] = ya
        m = (y_ref[:, s].astype(f32) + ya + skip_ref[:, s] * v).astype(bf16)
        mixer[:, s] = m
        z = z_ref[:, s].astype(f32)
        product = m.astype(f32) * (z * sigmoid(z))
        gated[:, s] = product
        squares = squares + product * product
        meets = meets + gn_ref[:, s].astype(f32) * gain_ref[:, s] * product
        tails[:, s] = (v * both[ROWS:, s]).astype(bf16)
    scale = lax.rsqrt(jnp.sum(squares, axis=1, keepdims=True) / width + epsilon)
    pull = scale * scale * scale * (jnp.sum(meets, axis=1, keepdims=True) / width)
    for i in range(pairs):
        s = slab(i)
        v = v_ref[:, s].astype(f32)
        product = gated[:, s]
        unit = product * scale
        gain = gain_ref[:, s]
        gn = gn_ref[:, s].astype(f32)
        out_ref[:, s] = (unit * gain).astype(bf16)
        ggain_ref[:, s] += jnp.sum(gn * unit, axis=0, keepdims=True)
        grad = gn * gain * scale - product * pull
        z = z_ref[:, s].astype(f32)
        sig = sigmoid(z)
        gm = (grad * (z * sig)).astype(bf16)
        gm_ref[:, s] = gm
        slope = sig * (1.0 + z * (1.0 - sig))
        gz_ref[:, s] = (grad * mixer[:, s].astype(f32) * slope).astype(bf16)
        g = gm.astype(f32)
        gskip_ref[:, s] += jnp.sum(g * v, axis=0, keepdims=True)
        products[:, s] = (g * across[:, s]).astype(bf16)
        early[:, s] = (g * both[:ROWS, s]).astype(bf16)
    pac_ref[...] = mm(products[...], ones_ref[...])
    back[...] += ebef_ref[pl.ds(at, 1), :] * mm_tn(c_ref[...], early[...])
    state[...] = etot_ref[pl.ds(at, 1), :] * state[...] + mm_tn(b_ref[...], tails[...])

    @pl.when(at == pl.num_programs(0) - 1)
    def _():
        back_ref[...] = back[...].astype(bf16)


def gate_both(y, act, z, gn, step, cum, etot, ebef, skip, gain, start, ones, fan, heads, inner, width):
    rows = act.shape[0]
    inputs_at = inner // width
    blocks = rows // ROWS
    return pl.pallas_call(
        functools.partial(gate_kernel, heads, inner // LANES),
        grid=(blocks,),
        in_specs=[
            by_rows(inner),
            by_rows(inner),
            pl.BlockSpec((ROWS, width), lambda i: (i, inputs_at)),
            pl.BlockSpec((ROWS, width), lambda i: (i, inputs_at + 1)),
            by_rows(inner),
            by_rows(inner),
            by_rows(LANES),
            by_rows(LANES),
            whole(etot.shape),
            whole(ebef.shape),
            whole((1, inner)),
            whole((1, inner)),
            whole((width, inner)),
            whole((inner, LANES)),
            whole(fan.shape),
        ],
        out_specs=[
            by_rows(inner),
            by_rows(inner),
            by_rows(inner),
            by_rows(inner, width),
            by_rows(LANES),
            whole((width, inner)),
            whole((1, inner)),
            whole((1, inner)),
        ],
        out_shape=[
            jax.ShapeDtypeStruct((rows, inner), bf16),
            jax.ShapeDtypeStruct((rows, inner), bf16),
            jax.ShapeDtypeStruct((rows, inner), bf16),
            jax.ShapeDtypeStruct((blocks * width, inner), bf16),
            jax.ShapeDtypeStruct((rows, LANES), f32),
            jax.ShapeDtypeStruct((width, inner), bf16),
            jax.ShapeDtypeStruct((1, inner), f32),
            jax.ShapeDtypeStruct((1, inner), f32),
        ],
        scratch_shapes=[
            pltpu.VMEM((width, inner), f32),
            pltpu.VMEM((width, inner), f32),
            pltpu.VMEM((ROWS, inner), f32),
            pltpu.VMEM((ROWS, inner), bf16),
            pltpu.VMEM((ROWS, inner), f32),
            pltpu.VMEM((ROWS, inner), bf16),
            pltpu.VMEM((ROWS, inner), bf16),
            pltpu.VMEM((ROWS, inner), bf16),
            pltpu.VMEM((2 * ROWS, inner), f32),
        ],
        compiler_params=params(),
        name="gate_both",
        cost_estimate=cost(18),
    )(y, act, act, act, z, gn, step, cum, etot, ebef, skip, gain, start, ones, fan)


def inside_back_kernel(
    pairs, x_ref, b_ref, c_ref, g_ref, left_ref, right_ref, still_ref, taken_ref,
    dx_ref, db_ref, dc_ref, pq_ref, right, moved, late,
):
    fixed = left_rows(right, still_ref, right_ref)
    lane = lanes_at()
    low, high = low_lanes()
    raw_scores = mm_nt(b_ref[...], c_ref[...])
    scores = jnp.where(rows_at() <= lane, raw_scores, 0.0)
    strict = jnp.where(rows_at() < lane, raw_scores, 0.0)
    scores = jnp.concatenate([scores, scores], axis=1)
    strict = jnp.concatenate([strict, strict], axis=1)
    left = -left_ref[...]
    gathered = jnp.zeros((ROWS, 2 * LANES), f32)
    for i in range(pairs):
        spread = mm(left, fixed[:, wide(i)])
        decay = jnp.exp2(jnp.minimum(spread, 0.0))
        stacked = diagonal(g_ref[:, slab(i)], low, high)
        grad = mm_nt(x_ref[:, slab(i)], stacked) * decay
        gathered = gathered + grad
        moved[:, wide(i)] = (grad * strict).astype(bf16)
        dx_ref[:, slab(i)] = mm((scores * decay).astype(bf16), stacked).astype(bf16)
    late[...] = jnp.zeros_like(late)
    ones = jnp.ones((16, ROWS), bf16)
    for i in range(pairs):
        sums = mm(ones, moved[:, wide(i)])
        late[2 * i : 2 * i + 1, :] = sums[0:1, :LANES]
        late[2 * i + 1 : 2 * i + 2, :] = sums[0:1, LANES:]
    pq_ref[...] = late[...].T - mm(moved[...], taken_ref[...])
    gathered = gathered[:, :LANES] + gathered[:, LANES:]
    gathered = jnp.where(rows_at() <= lane, gathered, 0.0).astype(bf16)
    db_ref[...] = mm(gathered, c_ref[...])
    dc_ref[...] = mm_tn(gathered, b_ref[...])


def inside_backward(x, act, gm, left, right, still, taken, inner, width):
    rows = act.shape[0]
    inputs_at = inner // width
    return pl.pallas_call(
        functools.partial(inside_back_kernel, inner // LANES),
        grid=(rows // ROWS,),
        in_specs=[
            by_rows(inner),
            pl.BlockSpec((ROWS, width), lambda i: (i, inputs_at)),
            pl.BlockSpec((ROWS, width), lambda i: (i, inputs_at + 1)),
            by_rows(inner),
            by_rows(LANES),
            by_rows(right.shape[1], HALO),
            whole(still.shape),
            whole(taken.shape),
        ],
        out_specs=[by_rows(inner), by_rows(width), by_rows(width), by_rows(LANES)],
        out_shape=[
            jax.ShapeDtypeStruct((rows, inner), bf16),
            jax.ShapeDtypeStruct((rows, width), f32),
            jax.ShapeDtypeStruct((rows, width), f32),
            jax.ShapeDtypeStruct((rows, LANES), f32),
        ],
        scratch_shapes=[
            pltpu.VMEM(still.shape, bf16),
            pltpu.VMEM((ROWS, 2 * inner), bf16),
            pltpu.VMEM((LANES, ROWS), f32),
        ],
        compiler_params=params(),
        name="inside_backward",
        cost_estimate=cost(20),
    )(x, act, act, gm, left, right, still, taken)


def finish_kernel(
    heads,
    pairs,
    blocks,
    v_ref,
    x_ref,
    b_ref,
    c_ref,
    g_ref,
    dx_ref,
    db_ref,
    dc_ref,
    pq_ref,
    pac_ref,
    states_ref,
    step_ref,
    cum_ref,
    raw_ref,
    bias_ref,
    alog_ref,
    etot_ref,
    skip_ref,
    start_ref,
    ones_ref,
    fan_ref,
    gact_ref,
    graw_ref,
    gbias_ref,
    grate_ref,
    state,
    tails,
    early,
    first,
    second,
    spread,
    three,
):
    at = pl.program_id(0)
    block = blocks - 1 - at
    inner = pairs * LANES
    width = state.shape[0]

    @pl.when(at == 0)
    def _():
        state[...] = start_ref[...]
        gbias_ref[...] = jnp.zeros_like(gbias_ref)
        grate_ref[...] = jnp.zeros_like(grate_ref)

    leaving = state[...]
    leaving_low = leaving.astype(bf16)
    entering = states_ref[...]
    etot = etot_ref[pl.ds(block, 1), :]
    held = jnp.sum(leaving * entering.astype(f32), axis=0, keepdims=True) * etot
    held = mm(jnp.broadcast_to(held, (8, inner)).astype(bf16), ones_ref[...])[0:1, :]
    spread[...] = mm(b_ref[...], leaving_low)
    cum, step = cum_ref[...], step_ref[...]
    grow = jnp.exp(cum)
    tail = jnp.exp(cum[ROWS - 1 :, :] - cum)
    three[...] = mm(
        jnp.concatenate([halves(step, heads), halves(tail, heads), halves(grow, heads)], axis=0), fan_ref[...]
    )
    for i in range(pairs):
        s = slab(i)
        v = v_ref[:, s].astype(f32)
        g = g_ref[:, s].astype(f32)
        steps = three[:ROWS, s]
        x = x_ref[:, s].astype(f32)
        part_tail = three[ROWS : 2 * ROWS, s]
        more = spread[:, s] * part_tail
        dx = dx_ref[:, s].astype(f32) + more
        first[:, s] = (x * more).astype(bf16)
        second[:, s] = (v * dx).astype(bf16)
        gact_ref[:, s] = (steps * dx + skip_ref[:, s] * g).astype(bf16)
        tails[:, s] = (x * part_tail).astype(bf16)
        early[:, s] = (g * three[2 * ROWS :, s]).astype(bf16)
    gact_ref[:, inner : inner + width] = (db_ref[...] + mm_nt(tails[...], leaving_low)).astype(bf16)
    gact_ref[:, inner + width :] = (dc_ref[...] + mm_nt(early[...], entering)).astype(bf16)
    later = (rows_at() <= lanes_at()).astype(f32)
    earlier = (rows_at() > lanes_at()).astype(f32)
    gdecay = (
        jnp.dot(later, pq_ref[...] + pac_ref[...], precision=highest, preferred_element_type=f32)
        + jnp.dot(
            earlier, mm(first[...], ones_ref[...]), precision=highest, preferred_element_type=f32
        )
        + held
    )
    gstep = mm(second[...], ones_ref[...]) - jnp.exp(alog_ref[...]) * gdecay
    graw = gstep.astype(bf16).astype(f32) * sigmoid(raw_ref[...] + bias_ref[...])
    graw_ref[...] = graw.astype(bf16)
    gbias_ref[...] += jnp.sum(graw, axis=0, keepdims=True)
    grate_ref[...] += jnp.sum(step * gdecay, axis=0, keepdims=True)
    state[...] = etot * leaving + mm_tn(c_ref[...], early[...])


def mixer_finish(
    act, x, gm, dx, db, dc, pq, pac, states, step, cum, raw, bias, a_log, etot, skip, start, ones, fan, heads, inner, width
):
    rows = act.shape[0]
    blocks = rows // ROWS
    inputs_at = inner // width
    channels = act.shape[1]

    def backwards(columns, height=ROWS, column_at=0):
        return pl.BlockSpec((height, columns), lambda i: (blocks - 1 - i, column_at))

    return pl.pallas_call(
        functools.partial(finish_kernel, heads, inner // LANES, blocks),
        grid=(blocks,),
        in_specs=[
            backwards(inner),
            backwards(inner),
            backwards(width, column_at=inputs_at),
            backwards(width, column_at=inputs_at + 1),
            backwards(inner),
            backwards(inner),
            backwards(width),
            backwards(width),
            backwards(LANES),
            backwards(LANES),
            backwards(inner, width),
            backwards(LANES),
            backwards(LANES),
            backwards(LANES),
            whole((1, LANES)),
            whole((1, LANES)),
            whole(etot.shape),
            whole((1, inner)),
            whole((width, inner)),
            whole((inner, LANES)),
            whole(fan.shape),
        ],
        out_specs=[backwards(channels), backwards(LANES), whole((1, LANES)), whole((1, LANES))],
        out_shape=[
            jax.ShapeDtypeStruct((rows, channels), bf16),
            jax.ShapeDtypeStruct((rows, LANES), bf16),
            jax.ShapeDtypeStruct((1, LANES), f32),
            jax.ShapeDtypeStruct((1, LANES), f32),
        ],
        scratch_shapes=[
            pltpu.VMEM((width, inner), f32),
            pltpu.VMEM((ROWS, inner), bf16),
            pltpu.VMEM((ROWS, inner), bf16),
            pltpu.VMEM((ROWS, inner), bf16),
            pltpu.VMEM((ROWS, inner), bf16),
            pltpu.VMEM((ROWS, inner), f32),
            pltpu.VMEM((3 * ROWS, inner), f32),
        ],
        compiler_params=params(),
        name="mixer_finish",
        cost_estimate=cost(16),
    )(act, x, act, act, gm, dx, db, dc, pq, pac, states, step, cum, raw, bias, a_log, etot, skip, start, ones, fan)


def conv_back_kernel(
    span, rows, blocks, cin_ref, gact_ref, graw_ref, taps_ref, bias_ref,
    gproj_ref, gtaps_ref, gbias_ref, top_ref, rest_ref, held, grads,
):
    part = 256
    at = pl.program_id(0)

    @pl.when(at == blocks)
    def _():
        gproj_ref[...] = graw_ref[...]

    @pl.when(at < blocks)
    def _():
        held[...] = cin_ref[...].astype(f32)
        grads[rows:, :] = jnp.zeros((HALO, LANES), f32)
        gbias = jnp.zeros((1, LANES), f32)
        gtaps = [jnp.zeros((1, LANES), f32)] * span
        for start in range(0, rows, part):
            total = jnp.broadcast_to(bias_ref[0:1, :], (part, LANES))
            seen = []
            for k in range(span):
                first = HALO + start - (span - 1) + k
                seen.append(held[first : first + part, :])
                total = total + taps_ref[k : k + 1, :] * seen[k]
            sig = sigmoid(total)
            grad = gact_ref[start : start + part, :].astype(f32) * (sig * (1.0 + total * (1.0 - sig)))
            grads[start : start + part, :] = grad
            gbias = gbias + jnp.sum(grad, axis=0, keepdims=True)
            for k in range(span):
                gtaps[k] = gtaps[k] + jnp.sum(seen[k] * grad, axis=0, keepdims=True)
        gbias_ref[...] = gbias
        for k in range(span):
            gtaps_ref[k : k + 1, :] = gtaps[k]
        top_ref[...] = grads[0:8, :]
        for start in range(0, rows, part):
            total = jnp.zeros((part, LANES), f32)
            for k in range(span):
                first = start + span - 1 - k
                total = total + taps_ref[k : k + 1, :] * grads[first : first + part, :]
            gproj_ref[start : start + part, :] = total.astype(bf16)
            if start + part == rows:
                rest_ref[...] = total[part - 8 :, :]


def conv_backward(cin, gact, graw, taps, bias):
    rows, channels = gact.shape
    blocks = channels // LANES
    span = taps.shape[0]

    def columns(height):
        return pl.BlockSpec((height, LANES), lambda i: (0, jnp.minimum(i, blocks - 1)))

    return pl.pallas_call(
        functools.partial(conv_back_kernel, span, rows, blocks),
        grid=(blocks + 1,),
        in_specs=[columns(rows + HALO), columns(rows), whole((rows, LANES)), columns(span), columns(1)],
        out_specs=[
            pl.BlockSpec((rows, LANES), lambda i: (0, i)),
            columns(span),
            columns(1),
            columns(8),
            columns(8),
        ],
        out_shape=[
            jax.ShapeDtypeStruct((rows, channels + LANES), bf16),
            jax.ShapeDtypeStruct((span, channels), f32),
            jax.ShapeDtypeStruct((1, channels), f32),
            jax.ShapeDtypeStruct((8, channels), f32),
            jax.ShapeDtypeStruct((8, channels), f32),
        ],
        scratch_shapes=[pltpu.VMEM((rows + HALO, LANES), f32), pltpu.VMEM((rows + HALO, LANES), f32)],
        compiler_params=params(),
        name="conv_backward",
        cost_estimate=cost(18),
    )(cin, gact, graw, taps, bias)


def local(
    tokens,
    norm_gain,
    in_weight,
    conv_weight,
    conv_bias,
    dt_bias,
    a_log,
    skip_gain,
    gate_gain,
    out_weight,
    cotangent,
):
    tokens, incoming = tokens[0], cotangent[0]
    rows, model = tokens.shape
    heads = a_log.shape[0]
    span, channels = conv_weight.shape
    inner = gate_gain.shape[0]
    width = (channels - inner) // 2
    head_width = inner // heads
    blocks = rows // ROWS
    pad = LANES - heads

    conv_part = jnp.pad(in_weight[:, inner:], ((0, 0), (0, pad)))
    w_conv = lax.all_gather(conv_part, "fsdp", axis=0, tiled=True)
    gate_part, w_conv = lax.optimization_barrier((in_weight[:, :inner], w_conv))
    w_gate = lax.all_gather(gate_part, "fsdp", axis=0, tiled=True)
    out_weight, w_gate = lax.optimization_barrier((out_weight, w_gate))
    w_out = lax.all_gather(out_weight, "fsdp", axis=0, tiled=True)

    before = shifted(tokens[rows - HALO :], "seq", 1)
    residual = jnp.concatenate([before, tokens], axis=0).astype(f32)
    scale = lax.rsqrt(jnp.mean(residual * residual, axis=1, keepdims=True) + epsilon)
    normed = (residual * scale * norm_gain).astype(bf16)
    act, cin = conv_forward(normed, w_conv, conv_weight, conv_bias[None])
    own = normed[HALO:]
    raw = mm(own, w_conv[:, channels:])
    bias_row = jnp.pad(dt_bias, (0, pad))[None]
    alog_row = jnp.pad(a_log, (0, pad))[None]
    step, cum, left, right = steps_forward(raw, bias_row, alog_row, heads)

    totals = cum.reshape(blocks, ROWS, LANES)[:, -1, :heads]
    befores = jnp.cumsum(totals, axis=0) - totals
    etot = jnp.repeat(jnp.exp(totals), head_width, axis=1)
    ebef = jnp.repeat(jnp.exp(befores), head_width, axis=1)
    skip = jnp.repeat(skip_gain, head_width)[None]
    ones = (
        lax.broadcasted_iota(jnp.int32, (inner, LANES), 0) // head_width
        == lax.broadcasted_iota(jnp.int32, (inner, LANES), 1)
    ).astype(bf16)

    def fanned(count, each):
        row = lax.broadcasted_iota(jnp.int32, (LANES, count), 0)
        column = lax.broadcasted_iota(jnp.int32, (LANES, count), 1)
        return ((row < 3 * heads) & (row % heads == column // each)).astype(bf16)

    fan = fanned(inner, head_width)
    still = fanned(heads * LANES, LANES)
    taken = (
        lax.broadcasted_iota(jnp.int32, (heads * LANES, LANES), 0) // LANES
        == lax.broadcasted_iota(jnp.int32, (heads * LANES, LANES), 1)
    ).astype(bf16)
    whole_decay = jnp.repeat(jnp.exp(jnp.sum(totals, axis=0)), head_width)[None]

    def handed_on(state, distance):
        entering = jnp.zeros(state.shape, f32)
        state = state.astype(f32)
        for _ in range(lax.axis_size("seq") - 1):
            leaving = (state + whole_decay * entering).astype(bf16)
            entering = shifted(leaving, "seq", distance).astype(f32)
        return entering

    x, leaves = piece_state(act, step, cum, etot, fan, heads, inner, width)
    start = handed_on(leaves, 1)
    y = inside_forward(x, act, left, right, still, inner, width)
    z = mm(own, w_gate).astype(bf16)
    gn = mm_nt(incoming, w_out).astype(bf16)
    out_in, gm, gz, states, pac, back, ggain, gskip = gate_both(
        y, act, z, gn, step, cum, etot, ebef, skip, gate_gain[None], start, ones, fan, heads, inner, width
    )
    back_start = handed_on(back, -1)
    mixed = (tokens.astype(f32) + mm(out_in, w_out)).astype(bf16)
    part_out = mm_tn(out_in, incoming).astype(bf16)
    part_gate = mm_tn(own, gz).astype(bf16)
    own_rows = model // (lax.axis_size("seq") * lax.axis_size("fsdp"))
    grad_out_weight = sum_scatter(part_out, own_rows * inner // model)
    grad_gate_weight = sum_scatter(part_gate, own_rows)
    grad_normed = mm_nt(gz, w_gate)

    dx, db, dc, pq = inside_backward(x, act, gm, left, right, still, taken, inner, width)
    gact, graw, gdt, grate = mixer_finish(
        act, x, gm, dx, db, dc, pq, pac, states, step, cum, raw, bias_row, alog_row, etot, skip,
        back_start, ones, fan, heads, inner, width,
    )
    gproj, gtaps, gcbias, top, rest = conv_backward(cin, gact, graw, conv_weight, conv_bias[None])
    nexts = shifted(top, "seq", -1)
    owed = jnp.zeros((8, channels), f32)
    for k in range(span - 1):
        reach = span - 1 - k
        owed = owed + jnp.pad(conv_weight[k] * nexts[:reach], ((8 - reach, 0), (0, 0)))
    gproj = lax.dynamic_update_slice(gproj, (rest + owed).astype(bf16), (rows - 8, 0))

    part_conv = mm_tn(own, gproj).astype(bf16)
    grad_conv_part = sum_scatter(part_conv, own_rows)
    grad_normed = grad_normed + mm_nt(gproj, w_conv)
    own_residual, own_scale = residual[HALO:], scale[HALO:]
    unit = own_residual * own_scale
    pulled = grad_normed * norm_gain
    mean_pull = jnp.mean(pulled * unit, axis=1, keepdims=True)
    grad_tokens = incoming.astype(f32) + own_scale * (pulled - unit * mean_pull)
    grad_norm_gain = jnp.sum(grad_normed * unit, axis=0)

    grad_in_weight = jnp.concatenate(
        [grad_gate_weight, grad_conv_part[:, : channels + heads]], axis=1
    )
    small = [
        gtaps.reshape(-1),
        gcbias[0],
        gdt[0, :heads],
        grate[0, :heads] * -jnp.exp(a_log),
        jnp.sum(gskip.reshape(heads, head_width), axis=1),
        ggain[0],
    ]
    sizes = [part.shape[0] for part in small]
    summed = sum_all(jnp.concatenate(small))
    grad_norm_gain = sum_all(grad_norm_gain)
    split, at = [], 0
    for size in sizes:
        split.append(summed[at : at + size])
        at += size
    return (
        mixed[None],
        grad_tokens[None],
        grad_in_weight,
        grad_out_weight,
        grad_norm_gain,
        split[0].reshape(span, channels),
        *split[1:],
    )


def solution(mesh):
    tokens = P("fsdp", "seq", None)
    sharded = P("fsdp", None)
    spread = P(("seq", "fsdp"), None)
    return jax.shard_map(
        local,
        mesh=mesh,
        in_specs=(tokens, P(), sharded, P(), P(), P(), P(), P(), P(), sharded, tokens),
        out_specs=(tokens, tokens, spread, spread, P(), P(), P(), P(), P(), P(), P()),
        check_vma=False,
    )
```

time: 1490 us -> 513 us (0.34)
  waiting for transfers between devices: 558 us -> 153 us
  matrix products: 372 us -> 61.1 us
  other arithmetic: 235 us -> 34.2 us
  local copies, waits for them, and re-layouts: 221 us -> 23.7 us
  Pallas kernels: 0 us -> 125 us
  starting transfers between devices: 33.1 us -> 91.2 us
  blocking collectives: 42.1 us -> 0 us
    dot_general x25 -> x9, matrix products: 372 us -> 61.1 us  [the longest x3 25.9 us: mm_nt(): lax.dot_general(a, b, (((1,), (1,)), ((), ())), preferred_element_type=f32)]
    all_to_all x6 -> x0, waiting for transfers between devices: 228 us -> none  [the longest x1 91.9 us: local(): lax.all_to_all(head_out.astype(jnp.bfloat16), 'seq', split_axis=0, concat...]
    unnamed x6 -> x3, waiting for transfers between devices: 171 us -> 0.05 us
    pallas_call x0 -> x8, Pallas kernels: none -> 125 us  [the longest x1 29.4 us: gate_both(): pl.pallas_call(functools.partial(gate_kernel, heads, inner // LANES), gri...]
    another operation x17 -> x1, other arithmetic: 92.3 us -> 0.02 us  [local(): befores = jnp.cumsum(totals, axis=0) - totals]
    ppermute x2 -> x51, starting transfers between devices: 4.68 us -> 91.1 us  [the longest x9 32.2 us: line_sum(): up = lax.ppermute(up + ahead, 'seq', [(i, i + 1) for i in range(t)])]
    ppermute x2 -> x51, waiting for transfers between devices: 0.01 us -> 84.6 us  [the longest x25 46.4 us: exchanged(): lax.ppermute(block, axis, [(i, i ^ bit) for i in range(lax.axis_size(axis...]
    unnamed x121 -> x105, local copies, waits for them, and re-layouts: 71.7 us -> 9.5 us
  transfers between devices with their start and end apart: 13 -> 54, of which waited for: 8 -> 22; matrix products, arithmetic and copies ran while one was open for 17% -> 19% of each run, Pallas kernels for 0% -> 19%
where the time goes in v1:
time: 513 us; the launch traced here: 504 us
  waiting for transfers between devices  153 us (30%)
  Pallas kernels  125 us (24%)
  starting transfers between devices  91.2 us (18%)
  matrix products  61.1 us (12%)
  other arithmetic  34.2 us (7%)
  local copies, waits for them, and re-layouts  23.7 us (5%)
  between operations  15.4 us (3%)
    ppermute x25, waiting for transfers between devices, exchanged(): lax.ppermute(block, axis, [(i, i ^ bit) for i in range(lax.axis_size(axis...  46.4 us
    all_gather x1, waiting for transfers between devices, local(): w_conv = lax.all_gather(conv_part, 'fsdp', axis=0, tiled=True)  41.6 us
    ppermute x9, starting transfers between devices, line_sum(): up = lax.ppermute(up + ahead, 'seq', [(i, i + 1) for i in range(t)])  32.2 us
    pallas_call x1, Pallas kernels, gate_both(): pl.pallas_call(functools.partial(gate_kernel, heads, inner // LANES), gri...  29.4 us
    ppermute x25, starting transfers between devices, exchanged(): lax.ppermute(block, axis, [(i, i ^ bit) for i in range(lax.axis_size(axis...  28.6 us
    all_gather x1, waiting for transfers between devices, local(): w_gate = lax.all_gather(gate_part, 'fsdp', axis=0, tiled=True)  27.1 us
    dot_general x3, matrix products, mm_nt(): lax.dot_general(a, b, (((1,), (1,)), ((), ())), preferred_element_type=f32)  25.9 us
    ppermute x8, waiting for transfers between devices, shifted(): return lax.ppermute(block, axis, route)  24.2 us
  transfers between devices with their start and end apart: 54, of which 22 were waited for; matrix products, arithmetic and copies ran while one was open for 19% of the time, Pallas kernels for 19%

profile of v1, /device:TPU:0, one launch (start us, length us, event | category | flops | bytes accessed | tf_op | source)
XLA Modules:
  0.0 504.2 jit_solution(5866820150130106420)
XLA Ops:
  11.6 41.6 %all-gather.4.cloned.1.call-done.weight_ref = bf16[1024,2432]{1,0:T(8,128)(2,1)} async-done(((bf16[128,2432]{1,0:T(8,128)(2,1)}), bf16[1024,2432]{1,0:T(8,128)(2,1)}) %all-gather.4.cloned.1.call-update) | async-done | bytes 4980752 | tf_op jit(solution)/shard_map/all_gather | solution.py:818
  66.1 27.1 %all-gather.6.cloned.1.call-done = bf16[1024,2048]{0,1:T(8,128)(2,1)} async-done(((bf16[128,2048]{0,1:T(8,128)(2,1)}), bf16[1024,2048]{0,1:T(8,128)(2,1)}) %all-gather.6.cloned.1.call-update) | async-done | bytes 4194320 | tf_op jit(solution)/shard_map/all_gather | solution.py:820
  93.6 16.5 %conv_forward.1 = (bf16[1024,2304]{1,0:T(8,128)(2,1)}, bf16[1040,2304]{1,0:T(8,128)(2,1)}) custom-call(bf16[1040,1024]{1,0:T(8,128)(2,1)S(1)} %multiply_convert_fusion.normed_ref, bf16[1024,2432]{1,0:T(8,128)(2,1)} %all-gather.4.cloned.1.call-done.weight_ref, f32[4,2304]{1,0:T(4,128)S(1)} %copy-done.6, f32[1,2304]{1,0:T(1,128)S(1)} %broadcast_in_dim.35.bias_ref), custom_call_target="tpu_custom_call" | custom-call | flops 14000000000 | bytes 4194304 | tf_op jit(solution)/shard_map/conv_forward/pallas_call | solution.py:167
  110.1 9.2 %piece_state.1 = (bf16[1024,2048]{1,0:T(8,128)(2,1)}, bf16[128,2048]{1,0:T(8,128)(2,1)S(1)}) custom-call(bf16[1024,2304]{1,0:T(8,128)(2,1)} %get-tuple-element.45.v_ref.b_ref.c_ref, bf16[1024,2304]{1,0:T(8,128)(2,1)} %get-tuple-element.45.v_ref.b_ref.c_ref, f32[1024,128]{1,0:T(8,128)S(1)} %copy-done.16, f32[1024,128]{1,0:T(8,128)S(1)} %copy-done.8, ...), custom_call_target="tpu_custom_call" | custom-call | flops 6000000000 | bytes 4194304 | tf_op jit(solution)/shard_map/piece_state/pallas_call | solution.py:263
  127.4 6.9 %collective-permute-done.1 = bf16[128,2048]{1,0:T(8,128)(2,1)S(1)} collective-permute-done((bf16[128,2048]{1,0:T(8,128)(2,1)S(1)}, bf16[128,2048]{1,0:T(8,128)(2,1)S(1)}, u32[]{:S(2)}, u32[]{:S(2)}) %collective-permute-start.1) | collective-permute-done | bytes 524320 | tf_op jit(solution)/shard_map/ppermute | solution.py:24
  160.0 10.8 %inside_forward.1.y_ref = bf16[1024,2048]{1,0:T(8,128)(2,1)} custom-call(bf16[1024,2048]{1,0:T(8,128)(2,1)} %get-tuple-element.48.x_ref, bf16[1024,2304]{1,0:T(8,128)(2,1)} %get-tuple-element.45.v_ref.b_ref.c_ref, bf16[1024,2304]{1,0:T(8,128)(2,1)} %get-tuple-element.45.v_ref.b_ref.c_ref, bf16[1024,128]{1,0:T(8,128)(2,1)S(1)} %copy-done.25, ...), custom_call_target="tpu_custom_call" | custom-call | flops 10000000000 | bytes 4194304 | tf_op jit(solution)/shard_map/inside_forward/pallas_call | solution.py:315
  171.8 6.2 %convolution_convert_fusion.3.z_ref = bf16[1024,2048]{1,0:T(8,128)(2,1)} fusion(bf16[1024,2048]{0,1:T(8,128)(2,1)S(1)} %copy-done.41, bf16[1040,1024]{1,0:T(8,128)(2,1)S(1)} %multiply_convert_fusion.normed_ref), kind=kOutput, calls=%fused_computation.11 | convolution fusion | flops 4297064448 | bytes 10485760 | tf_op jit(solution)/shard_map/dot_general | solution.py:86
  178.0 9.5 %convert_bitcast_fusion.gn_ref = bf16[1024,2048]{1,0:T(8,128)(2,1)} fusion(bf16[2048,1024]{1,0:T(8,128)(2,1)} %all-gather.8.cloned.1.call-done, bf16[1,1024,1024]{2,1,0:T(8,128)(2,1)} %param.21), kind=kOutput, calls=%fused_computation.8 | convolution fusion | flops 4297064448 | bytes 10485760 | tf_op jit(solution)/shard_map/dot_general | solution.py:90
  187.6 29.4 %gate_both.1 = (bf16[1024,2048]{1,0:T(8,128)(2,1)}, bf16[1024,2048]{1,0:T(8,128)(2,1)}, bf16[1024,2048]{1,0:T(8,128)(2,1)}, bf16[1024,2048]{1,0:T(8,128)(2,1)}, ...) custom-call(bf16[1024,2048]{1,0:T(8,128)(2,1)} %inside_forward.1.y_ref, ...), custom_call_target="tpu_custom_call" | custom-call | flops 17999998976 | bytes 4194304 | tf_op jit(solution)/shard_map/gate_both/pallas_call | solution.py:438
  219.6 8.4 %convolution_convert_fusion.1 = bf16[2048,1024]{1,0:T(8,128)(2,1)} fusion(bf16[1024,2048]{1,0:T(8,128)(2,1)} %get-tuple-element.55, bf16[1,1024,1024]{2,1,0:T(8,128)(2,1)S(1)} %copy-done.33), kind=kOutput, calls=%fused_computation.9 | convolution fusion | flops 4297064448 | bytes 10485760 | tf_op jit(solution)/shard_map/dot_general | solution.py:94
  242.2 8.9 %collective-permute-done.5 = bf16[128,2048]{1,0:T(8,128)(2,1)S(1)} collective-permute-done((bf16[128,2048]{1,0:T(8,128)(2,1)S(1)}, bf16[128,2048]{1,0:T(8,128)(2,1)S(1)}, u32[]{:S(2)}, u32[]{:S(2)}) %collective-permute-start.5) | collective-permute-done | bytes 524320 | tf_op jit(solution)/shard_map/ppermute | solution.py:24
  252.6 20.6 %inside_backward.1 = (bf16[1024,2048]{1,0:T(8,128)(2,1)}, f32[1024,128]{1,0:T(8,128)S(1)}, f32[1024,128]{1,0:T(8,128)S(1)}, f32[1024,128]{1,0:T(8,128)S(1)}) custom-call(bf16[1024,2048]{1,0:T(8,128)(2,1)} %get-tuple-element.48.x_ref, bf16[1024,2304]{1,0:T(8,128)(2,1)} %get-tuple-element.45.v_ref.b_ref.c_ref, ...), custom_call_target="tpu_custom_call" | custom-call | flops 20000000000 | bytes 4194304 | tf_op jit(solution)/shard_map/inside_backward/pallas_call | solution.py:533
  273.3 19.6 %mixer_finish.1 = (bf16[1024,2304]{1,0:T(8,128)(2,1)}, bf16[1024,128]{1,0:T(8,128)(2,1)S(1)}, f32[1,128]{1,0:T(1,128)S(1)}, f32[1,128]{1,0:T(1,128)S(1)}) custom-call(bf16[1024,2304]{1,0:T(8,128)(2,1)} %get-tuple-element.45.v_ref.b_ref.c_ref, bf16[1024,2048]{1,0:T(8,128)(2,1)} %get-tuple-element.48.x_ref, ...), custom_call_target="tpu_custom_call" | custom-call | flops 16000000000 | bytes 4194304 | tf_op jit(solution)/shard_map/mixer_finish/pallas_call | solution.py:669
  295.3 18.0 %conv_backward.1 = (bf16[1024,2432]{1,0:T(8,128)(2,1)}, f32[4,2304]{1,0:T(4,128)S(1)}, f32[1,2304]{1,0:T(1,128)S(1)}, f32[8,2304]{1,0:T(8,128)S(1)}, f32[8,2304]{1,0:T(8,128)S(1)}) custom-call(bf16[1040,2304]{1,0:T(8,128)(2,1)} %get-tuple-element.57.cin_ref, bf16[1024,2304]{1,0:T(8,128)(2,1)S(1)} %copy-done.14, ...), custom_call_target="tpu_custom_call" | custom-call | flops 17999998976 | bytes 4194304 | tf_op jit(solution)/shard_map/conv_backward/pallas_call | solution.py:769
  320.9 9.1 %fusion.89 = f32[1024,1024]{1,0:T(8,128)S(1)} fusion(bf16[1024,2432]{1,0:T(8,128)(2,1)} %fusion.78, bf16[1024,2432]{1,0:T(8,128)(2,1)} %all-gather.4.cloned.1.call-done.weight_ref), kind=kOutput, calls=%fused_computation.217 | convolution fusion | flops 5100273664 | bytes 14155776 | tf_op jit(solution)/shard_map/dot_general | solution.py:90
  330.1 7.3 %multiply_reduce_fusion.1 = (f32[1024]{0:T(1024)S(1)}, f32[1024]{0:T(1024)S(1)}, f32[1024,1024]{1,0:T(8,128)S(1)}) fusion(f32[1040,1024]{1,0:T(8,128)} %maximum_convert_fusion, f32[1024]{0:T(1024)S(1)} %slice.123, f32[1024]{0:T(1024)S(1)} %copy-done.36, f32[1024,1024]{1,0:T(8,128)S(1)} %fusion.89, bf16[1024,2048]{1,0:T(8,128)(2,1)S(1)} %copy-done.45, ...), kind=kOutput, calls=%fused_computation.4 | convolution fusion | flops 4302305280 | bytes 20987904 | tf_op jit(solution)/shard_map/dot_general | solution.py:90
  337.5 8.1 %fusion = bf16[1,1024,1024]{2,1,0:T(8,128)(2,1)} fusion(bf16[1024,2048]{1,0:T(8,128)(2,1)} %get-tuple-element.55, bf16[2048,1024]{1,0:T(8,128)(2,1)S(1)} %copy-done.43, bf16[1,1024,1024]{2,1,0:T(8,128)(2,1)S(1)} %copy-done.29), kind=kOutput, calls=%fused_computation.15 | convolution fusion | flops 4298113024 | bytes 12582912 | tf_op jit(solution)/shard_map/dot_general | solution.py:86
  347.8 6.1 %convolution_convert_fusion = bf16[1024,2432]{1,0:T(8,128)(2,1)S(1)} fusion(bf16[1024,2432]{1,0:T(8,128)(2,1)S(1)} %bitcast.212, bf16[1040,1024]{1,0:T(8,128)(2,1)S(1)} %multiply_convert_fusion.normed_ref), kind=kOutput, calls=%fused_computation | convolution fusion | flops 5102764032 | bytes 12058624 | tf_op jit(solution)/shard_map/dot_general | solution.py:94
  382.6 8.0 %collective-permute-done.33 = bf16[4,2,32,1024]{3,2,1,0:T(8,128)(2,1)S(1)} collective-permute-done((bf16[4,2,32,1024]{3,2,1,0:T(8,128)(2,1)S(1)}, bf16[4,2,32,1024]{3,2,1,0:T(8,128)(2,1)S(1)}, u32[]{:S(2)}, u32[]{:S(2)}) %collective-permute-start.33) | collective-permute-done | bytes 524320 | tf_op jit(solution)/shard_map/ppermute | solution.py:28
  393.7 8.1 %collective-permute-done.11 = bf16[4,2,16,2048]{3,2,1,0:T(8,128)(2,1)S(1)} collective-permute-done((bf16[4,2,16,2048]{3,2,1,0:T(8,128)(2,1)S(1)}, bf16[4,2,16,2048]{3,2,1,0:T(8,128)(2,1)S(1)}, u32[]{:S(2)}, u32[]{:S(2)}) %collective-permute-start.11) | collective-permute-done | bytes 524320 | tf_op jit(solution)/shard_map/ppermute | solution.py:28
  441.0 11.6 %collective-permute-done.20 = bf16[4,2,16,2432]{3,2,1,0:T(8,128)(2,1)S(1)} collective-permute-done((bf16[4,2,16,2432]{3,2,1,0:T(8,128)(2,1)S(1)}, bf16[4,2,16,2432]{3,2,1,0:T(8,128)(2,1)S(1)}, u32[]{:S(2)}, u32[]{:S(2)}) %collective-permute-start.20) | collective-permute-done | bytes 622624 | tf_op jit(solution)/shard_map/ppermute | solution.py:28
  453.8 5.8 %collective-permute-done.23 = bf16[4,16,2432]{2,1,0:T(8,128)(2,1)S(1)} collective-permute-done((bf16[4,16,2432]{2,1,0:T(8,128)(2,1)S(1)}, bf16[4,16,2432]{2,1,0:T(8,128)(2,1)S(1)}, u32[]{:S(2)}, u32[]{:S(2)}) %collective-permute-start.23) | collective-permute-done | bytes 311328 | tf_op jit(solution)/shard_map/ppermute | solution.py:28
  460.7 5.8 %collective-permute-done.21 = bf16[4,16,2432]{2,1,0:T(8,128)(2,1)S(1)} collective-permute-done((bf16[4,16,2432]{2,1,0:T(8,128)(2,1)S(1)}, bf16[4,16,2432]{2,1,0:T(8,128)(2,1)S(1)}, u32[]{:S(2)}, u32[]{:S(2)}) %collective-permute-start.21) | collective-permute-done | bytes 311328 | tf_op jit(solution)/shard_map/ppermute | solution.py:28
  491.2 5.4 %collective-permute-done.29 = bf16[32,2432]{1,0:T(8,128)(2,1)S(1)} collective-permute-done((bf16[32,2432]{1,0:T(8,128)(2,1)S(1)}, bf16[32,2432]{1,0:T(8,128)(2,1)S(1)}, u32[]{:S(2)}, u32[]{:S(2)}) %collective-permute-start.29) | collective-permute-done | bytes 155680 | tf_op jit(solution)/shard_map/ppermute | solution.py:44
  (333 shorter events, 181.0 us)
Async XLA Ops:
  7.2 46.0 %all-gather.4.cloned.1.call-start = ((), (), s32[]{:S(2)}) async-start(), calls=%async_computation | async-start | bytes 5603328 | tf_op jit(solution)/shard_map/all_gather | solution.py:818
  9.7 83.5 %all-gather.6.cloned.1.call-start = ((), (), s32[]{:S(2)}) async-start(), calls=%async_computation.1 | async-start | bytes 4718592 | tf_op jit(solution)/shard_map/all_gather | solution.py:820
  53.3 124.7 %all-gather.8.cloned.1.call-start = ((), (), s32[]{:S(2)}) async-start(), calls=%async_computation.2 | async-start | bytes 4718592 | tf_op jit(solution)/shard_map/all_gather | solution.py:822
  119.4 15.0 %collective-permute-start.1 = (bf16[128,2048]{1,0:T(8,128)(2,1)S(1)}, bf16[128,2048]{1,0:T(8,128)(2,1)S(1)}, u32[]{:S(2)}, u32[]{:S(2)}) collective-permute-start(bf16[128,2048]{1,0:T(8,128)(2,1)S(1)} %fusion.11), channel_id=1, source_target_pairs={{0,8},{8,16},{16,24},{1,9},{9,17},{17,25},{2,10},{10,18},{18,26},{... | collective-permute-start | bytes 1572872 | tf_op jit(solution)/shard_map/ppermute | solution.py:24
  135.3 15.5 %collective-permute-start.2 = (bf16[128,2048]{1,0:T(8,128)(2,1)}, bf16[128,2048]{1,0:T(8,128)(2,1)}, u32[]{:S(2)}, u32[]{:S(2)}) collective-permute-start(bf16[128,2048]{1,0:T(8,128)(2,1)} %fusion.12), channel_id=1, source_target_pairs={{0,8},{8,16},{16,24},{1,9},{9,17},{17,25},{2,10},{10,18},{18,26},{... | collective-permute-start | bytes 1572872 | tf_op jit(solution)/shard_map/ppermute | solution.py:24
  151.9 18.8 %collective-permute-start.3 = (bf16[128,2048]{1,0:T(8,128)(2,1)S(1)}, bf16[128,2048]{1,0:T(8,128)(2,1)S(1)}, u32[]{:S(2)}, u32[]{:S(2)}) collective-permute-start(bf16[128,2048]{1,0:T(8,128)(2,1)S(1)} %fusion.13), channel_id=1, source_target_pairs={{0,8},{8,16},{16,24},{1,9},{9,17},{17,25},{2,10},{10,18},{18,26},{... | collective-permute-start | bytes 1572872 | tf_op jit(solution)/shard_map/ppermute | solution.py:24
  232.7 140.2 %collective-permute-start.30 = (bf16[4,4,64,1024]{3,2,1,0:T(8,128)(2,1)}, bf16[4,4,64,1024]{3,2,1,0:T(8,128)(2,1)}, u32[]{:S(2)}, u32[]{:S(2)}) collective-permute-start(bf16[4,4,64,1024]{3,2,1,0:T(8,128)(2,1)} %dynamic-slice_bitcast_fusion.1), channel_id=1, source_target_pairs={{0,1},{1,0},{2,3},{3,2},{4,5},{5,4},{6,7},{7,6},{8,9},{9,8},{10,11... | collective-permute-start | bytes 6291464 | tf_op jit(solution)/shard_map/ppermute | solution.py:28
  233.9 17.1 %collective-permute-start.5 = (bf16[128,2048]{1,0:T(8,128)(2,1)S(1)}, bf16[128,2048]{1,0:T(8,128)(2,1)S(1)}, u32[]{:S(2)}, u32[]{:S(2)}) collective-permute-start(bf16[128,2048]{1,0:T(8,128)(2,1)S(1)} %fusion.15), channel_id=1, source_target_pairs={{8,0},{16,8},{24,16},{9,1},{17,9},{25,17},{10,2},{18,10},{26,18},{... | collective-permute-start | bytes 1572872 | tf_op jit(solution)/shard_map/ppermute | solution.py:24
  241.7 136.9 %collective-permute-start.8 = (bf16[4,4,32,2048]{3,2,1,0:T(8,128)(2,1)}, bf16[4,4,32,2048]{3,2,1,0:T(8,128)(2,1)}, u32[]{:S(2)}, u32[]{:S(2)}) collective-permute-start(bf16[4,4,32,2048]{3,2,1,0:T(8,128)(2,1)} %dynamic-slice_bitcast_fusion.2), channel_id=1, source_target_pairs={{0,1},{1,0},{2,3},{3,2},{4,5},{5,4},{6,7},{7,6},{8,9},{9,8},{10,11... | collective-permute-start | bytes 6291464 | tf_op jit(solution)/shard_map/ppermute | solution.py:28
  251.2 22.0 %collective-permute-start.6 = (bf16[128,2048]{1,0:T(8,128)(2,1)S(1)}, bf16[128,2048]{1,0:T(8,128)(2,1)S(1)}, u32[]{:S(2)}, u32[]{:S(2)}) collective-permute-start(bf16[128,2048]{1,0:T(8,128)(2,1)S(1)} %fusion.16), channel_id=1, source_target_pairs={{8,0},{16,8},{24,16},{9,1},{17,9},{25,17},{10,2},{18,10},{26,18},{... | collective-permute-start | bytes 1572872 | tf_op jit(solution)/shard_map/ppermute | solution.py:24
  314.9 30.7 %collective-permute-start.46 = (f32[13664]{0:T(1024)S(1)}, f32[13664]{0:T(1024)S(1)}, u32[]{:S(2)}, u32[]{:S(2)}) collective-permute-start(f32[13664]{0:T(1024)S(1)} %concatenate.23), channel_id=1, source_target_pairs={{0,1},{1,0},{2,3},{3,2},{4,5},{5,4},{6,7},{7,6},{8,9},{9,8},{10,11... | collective-permute-start | bytes 163976 | tf_op jit(solution)/shard_map/ppermute | solution.py:28
  356.3 70.9 %collective-permute-start.19 = (bf16[4,4,32,2432]{3,2,1,0:T(8,128)(2,1)S(1)}, bf16[4,4,32,2432]{3,2,1,0:T(8,128)(2,1)}, u32[]{:S(2)}, u32[]{:S(2)}) collective-permute-start(bf16[4,4,32,2432]{3,2,1,0:T(8,128)(2,1)S(1)} %dynamic-slice_bitcast_fusion), channel_id=1, source_target_pairs={{0,1},{1,0},{2,3},{3,2},{4,5},{5,4},{6,7},{7,6},{8,9},{9,8},{10,11... | collective-permute-start | bytes 7471112 | tf_op jit(solution)/shard_map/ppermute | solution.py:28
  375.7 14.9 %collective-permute-start.33 = (bf16[4,2,32,1024]{3,2,1,0:T(8,128)(2,1)S(1)}, bf16[4,2,32,1024]{3,2,1,0:T(8,128)(2,1)S(1)}, u32[]{:S(2)}, u32[]{:S(2)}) collective-permute-start(bf16[4,2,32,1024]{3,2,1,0:T(8,128)(2,1)S(1)} %dynamic-slice_bitcast_fusion.5), channel_id=1, source_target_pairs={{0,4},{1,5},{2,6},{3,7},{4,0},{5,1},{6,2},{7,3},{8,12},{9,13},{10,... | collective-permute-start | bytes 1572872 | tf_op jit(solution)/shard_map/ppermute | solution.py:28
  376.9 15.1 %collective-permute-start.31 = (bf16[4,2,32,1024]{3,2,1,0:T(8,128)(2,1)S(1)}, bf16[4,2,32,1024]{3,2,1,0:T(8,128)(2,1)S(1)}, u32[]{:S(2)}, u32[]{:S(2)}) collective-permute-start(bf16[4,2,32,1024]{3,2,1,0:T(8,128)(2,1)S(1)} %dynamic-slice_bitcast_fusion.6), channel_id=1, source_target_pairs={{0,2},{1,3},{2,0},{3,1},{4,6},{5,7},{6,4},{7,5},{8,10},{9,11},{10,... | collective-permute-start | bytes 1572872 | tf_op jit(solution)/shard_map/ppermute | solution.py:28
  380.7 21.1 %collective-permute-start.11 = (bf16[4,2,16,2048]{3,2,1,0:T(8,128)(2,1)S(1)}, bf16[4,2,16,2048]{3,2,1,0:T(8,128)(2,1)S(1)}, u32[]{:S(2)}, u32[]{:S(2)}) collective-permute-start(bf16[4,2,16,2048]{3,2,1,0:T(8,128)(2,1)S(1)} %dynamic-slice_bitcast_fusion.7), channel_id=1, source_target_pairs={{0,4},{1,5},{2,6},{3,7},{4,0},{5,1},{6,2},{7,3},{8,12},{9,13},{10,... | collective-permute-start | bytes 1572872 | tf_op jit(solution)/shard_map/ppermute | solution.py:28
  381.3 21.9 %collective-permute-start.9 = (bf16[4,2,16,2048]{3,2,1,0:T(8,128)(2,1)S(1)}, bf16[4,2,16,2048]{3,2,1,0:T(8,128)(2,1)S(1)}, u32[]{:S(2)}, u32[]{:S(2)}) collective-permute-start(bf16[4,2,16,2048]{3,2,1,0:T(8,128)(2,1)S(1)} %dynamic-slice_bitcast_fusion.8), channel_id=1, source_target_pairs={{0,2},{1,3},{2,0},{3,1},{4,6},{5,7},{6,4},{7,5},{8,10},{9,11},{10,... | collective-permute-start | bytes 1572872 | tf_op jit(solution)/shard_map/ppermute | solution.py:28
  390.7 16.6 %collective-permute-start.34 = (bf16[4,32,1024]{2,1,0:T(8,128)(2,1)S(1)}, bf16[4,32,1024]{2,1,0:T(8,128)(2,1)S(1)}, u32[]{:S(2)}, u32[]{:S(2)}) collective-permute-start(bf16[4,32,1024]{2,1,0:T(8,128)(2,1)S(1)} %dynamic-slice_bitcast_fusion.11), channel_id=1, source_target_pairs={{0,2},{1,3},{2,0},{3,1},{4,6},{5,7},{6,4},{7,5},{8,10},{9,11},{10,... | collective-permute-start | bytes 786440 | tf_op jit(solution)/shard_map/ppermute | solution.py:28
  392.1 15.2 %collective-permute-start.32 = (bf16[4,32,1024]{2,1,0:T(8,128)(2,1)S(1)}, bf16[4,32,1024]{2,1,0:T(8,128)(2,1)S(1)}, u32[]{:S(2)}, u32[]{:S(2)}) collective-permute-start(bf16[4,32,1024]{2,1,0:T(8,128)(2,1)S(1)} %dynamic-slice_bitcast_fusion.12), channel_id=1, source_target_pairs={{0,4},{1,5},{2,6},{3,7},{4,0},{5,1},{6,2},{7,3},{8,12},{9,13},{10,... | collective-permute-start | bytes 786440 | tf_op jit(solution)/shard_map/ppermute | solution.py:28
  412.5 18.3 %collective-permute-start.16 = (bf16[32,2048]{1,0:T(8,128)(2,1)S(1)}, bf16[32,2048]{1,0:T(8,128)(2,1)S(1)}, u32[]{:S(2)}, u32[]{:S(2)}) collective-permute-start(bf16[32,2048]{1,0:T(8,128)(2,1)S(1)} %get-tuple-element.99), channel_id=1, source_target_pairs={{24,16},{25,17},{26,18},{27,19},{28,20},{29,21},{30,22},{31,23}} | collective-permute-start | bytes 393224 | tf_op jit(solution)/shard_map/ppermute | solution.py:44
  421.6 49.6 %collective-permute-start.39 = (bf16[64,1024]{1,0:T(8,128)(2,1)S(1)}, bf16[64,1024]{1,0:T(8,128)(2,1)S(1)}, u32[]{:S(2)}, u32[]{:S(2)}) collective-permute-start(bf16[64,1024]{1,0:T(8,128)(2,1)S(1)} %get-tuple-element.93), channel_id=1, source_target_pairs={{24,16},{16,8},{25,17},{17,9},{26,18},{18,10},{27,19},{19,11},{28,... | collective-permute-start | bytes 393224 | tf_op jit(solution)/shard_map/ppermute | solution.py:44
  422.2 67.6 %collective-permute-start.37 = (bf16[64,1024]{1,0:T(8,128)(2,1)S(1)}, bf16[64,1024]{1,0:T(8,128)(2,1)S(1)}, u32[]{:S(2)}, u32[]{:S(2)}) collective-permute-start(bf16[64,1024]{1,0:T(8,128)(2,1)S(1)} %get-tuple-element.92), channel_id=1, source_target_pairs={{0,8},{8,16},{16,24},{1,9},{9,17},{17,25},{2,10},{10,18},{18,26},{... | collective-permute-start | bytes 393224 | tf_op jit(solution)/shard_map/ppermute | solution.py:43
  430.9 43.7 %collective-permute-start.17 = (bf16[32,2048]{1,0:T(8,128)(2,1)S(1)}, bf16[32,2048]{1,0:T(8,128)(2,1)S(1)}, u32[]{:S(2)}, u32[]{:S(2)}) collective-permute-start(bf16[32,2048]{1,0:T(8,128)(2,1)S(1)} %get-tuple-element.97), channel_id=1, source_target_pairs={{24,16},{16,8},{25,17},{17,9},{26,18},{18,10},{27,19},{19,11},{28,... | collective-permute-start | bytes 393224 | tf_op jit(solution)/shard_map/ppermute | solution.py:44
  431.5 50.9 %collective-permute-start.15 = (bf16[32,2048]{1,0:T(8,128)(2,1)S(1)}, bf16[32,2048]{1,0:T(8,128)(2,1)S(1)}, u32[]{:S(2)}, u32[]{:S(2)}) collective-permute-start(bf16[32,2048]{1,0:T(8,128)(2,1)S(1)} %get-tuple-element.96), channel_id=1, source_target_pairs={{0,8},{8,16},{16,24},{1,9},{9,17},{17,25},{2,10},{10,18},{18,26},{... | collective-permute-start | bytes 393224 | tf_op jit(solution)/shard_map/ppermute | solution.py:43
  471.2 18.6 %collective-permute-start.40 = (bf16[64,1024]{1,0:T(8,128)(2,1)S(1)}, bf16[64,1024]{1,0:T(8,128)(2,1)S(1)}, u32[]{:S(2)}, u32[]{:S(2)}) collective-permute-start(bf16[64,1024]{1,0:T(8,128)(2,1)S(1)} %fusion.44), channel_id=1, source_target_pairs={{24,16},{16,8},{8,0},{25,17},{17,9},{9,1},{26,18},{18,10},{10,2},{... | collective-permute-start | bytes 393224 | tf_op jit(solution)/shard_map/ppermute | solution.py:44
  (82 other events, 1073.6 us)
Sparse Core Ops, SparseCore 0:
  10.5 42.7 all-gather.3
  55.7 37.4 all-gather.5
  95.1 36.7 all-gather.7
